TPU v7x, 256 devices: a whole 4x4x8 slice. The times are simulated.
256 devices in a mesh: prefix: 32 (over x, z), kvhead: 8 (over y, core).
Axes of the slice: x: 4, y: 4, z: 8, core: 2. Of those that a mesh axis runs over, the one named last changes fastest.
Arguments:
- queries: bfloat16 [256, 8192], P('prefix', 'kvhead')
- prefix_keys: bfloat16 [262144, 1024], P('prefix', 'kvhead')
- prefix_values: bfloat16 [262144, 1024], P('prefix', 'kvhead'), may hold values from -6 to 6
- suffix_keys: bfloat16 [256, 1024, 1024], P('prefix', None, 'kvhead'), may hold values from -12 to 12
- suffix_values: bfloat16 [256, 1024, 1024], P('prefix', None, 'kvhead'), may hold values from -6 to 6
- suffix_lengths: int32 [256], replicated, may hold values from 1 to 1024, 131072 in all
- slot_request: int32 [256], P('prefix'), may hold values from 0 to 255, each once
- out_weight: bfloat16 [8192, 8192], P('kvhead', 'prefix'), may hold values from -0.0625 to 0.0625
Outputs:
- mixed: bfloat16 [256, 8192], P('kvhead', 'prefix')
Inputs may be any that keep to these rules, and one draw needn't show every extreme that they name: `suffix_lengths`: at least one continuation (in practice many) has all 1024 positions live; the others have uneven lengths. `slot_request`: each continuation sits in exactly one slot.
All inputs are finite; a program needn't handle non-finite values.
Results may differ from a plain program's by a relative error of at most 0.0065.
Values may be sent and summed in bfloat16 or wider, within the bound.
No kernel may reach another device: no remote copies, remote signals or barrier semaphores. Data moves between devices by JAX's collectives and lax.ppermute only.
A program may use at most 64 MiB of HBM per device.

v0:
```python
import math

import jax
import jax.numpy as jnp
from jax import lax
from jax.sharding import PartitionSpec as P

HEAD_DIM = 128
GROUP = 8


def on_device(
    queries,
    prefix_keys,
    prefix_values,
    suffix_keys,
    suffix_values,
    suffix_lengths,
    slot_request,
    out_weight,
):
    score_scale = HEAD_DIM ** (-0.5)
    owners = lax.axis_size("prefix")
    local_reqs = queries.shape[0]
    batch = local_reqs * owners
    heads_kv = prefix_keys.shape[1] // HEAD_DIM
    seg_len = prefix_keys.shape[0]
    span = suffix_keys.shape[1]
    everyone = lax.all_gather(queries, "prefix", axis=0, tiled=True)
    rows = batch * GROUP
    q_heads = (
        everyone.reshape(batch, heads_kv, GROUP, HEAD_DIM)
        .transpose(1, 0, 2, 3)
        .reshape(heads_kv, rows, HEAD_DIM)
    )
    block = math.gcd(rows, max(8, 512 // heads_kv))
    count = rows // block
    q_blocks = q_heads.reshape(heads_kv, count, block, HEAD_DIM).transpose(1, 0, 2, 3)
    keys = prefix_keys.reshape(seg_len, heads_kv, HEAD_DIM)
    values = prefix_values.reshape(seg_len, heads_kv, HEAD_DIM)

    def segment_part(q_block):
        scores = (
            jnp.einsum("gre,sge->grs", q_block, keys, preferred_element_type=jnp.float32)
            * score_scale
        )
        peak = jnp.max(scores, axis=-1)
        probs = jnp.exp(scores - peak[..., None]).astype(jnp.bfloat16)
        total = jnp.sum(probs, axis=-1, dtype=jnp.float32)
        numer = jnp.einsum("grs,sge->gre", probs, values, preferred_element_type=jnp.float32)
        ctx = (numer / total[..., None]).astype(jnp.bfloat16)
        return (peak, total, ctx)

    peak, total, seg_ctx = lax.map(segment_part, q_blocks)
    peak = peak.transpose(1, 0, 2).reshape(heads_kv, batch, GROUP).transpose(1, 0, 2)
    total = total.transpose(1, 0, 2).reshape(heads_kv, batch, GROUP).transpose(1, 0, 2)
    seg_ctx = (
        seg_ctx.transpose(1, 0, 2, 3)
        .reshape(heads_kv, batch, GROUP, HEAD_DIM)
        .transpose(1, 0, 2, 3)
    )
    start = lax.axis_index("prefix") * local_reqs
    top_all = lax.pmax(peak, "prefix")
    weights = jnp.exp(peak - top_all) * total
    scaled = (seg_ctx.astype(jnp.float32) * weights[..., None]).reshape(
        batch, heads_kv * GROUP * HEAD_DIM
    )
    pre_numer, pre_total = (
        lax.psum_scatter(scaled, "prefix", scatter_dimension=0, tiled=True),
        lax.psum_scatter(weights, "prefix", scatter_dimension=0, tiled=True),
    )
    pre_numer = pre_numer.reshape(local_reqs, heads_kv, GROUP, HEAD_DIM)
    top = lax.dynamic_slice_in_dim(top_all, start, local_reqs, 0)
    matches = slot_request[:, None] == jnp.arange(batch, dtype=jnp.int32)[None, :]
    my_len = jnp.sum(jnp.where(matches, suffix_lengths[None, :], 0), axis=1)
    live = (jnp.arange(span, dtype=jnp.int32)[None, :] < my_len[:, None])[:, None, None, :]
    own_q = queries.reshape(local_reqs, heads_kv, GROUP, HEAD_DIM)
    own_keys = suffix_keys.reshape(local_reqs, span, heads_kv, HEAD_DIM)
    own_values = suffix_values.reshape(local_reqs, span, heads_kv, HEAD_DIM)
    suf = (
        jnp.einsum("rghe,rsge->rghs", own_q, own_keys, preferred_element_type=jnp.float32)
        * score_scale
    )
    suf = jnp.where(live, suf, jnp.float32(-1e30))
    suf_max = jnp.max(suf, axis=-1)
    suf_prob = jnp.where(live, jnp.exp(suf - suf_max[..., None]), jnp.float32(0.0)).astype(
        jnp.bfloat16
    )
    suf_total = jnp.sum(suf_prob, axis=-1, dtype=jnp.float32)
    suf_num = jnp.einsum(
        "rghs,rsge->rghe", suf_prob, own_values, preferred_element_type=jnp.float32
    )
    best = jnp.maximum(top, suf_max)
    from_prefix = jnp.exp(top - best)
    from_suffix = jnp.exp(suf_max - best)
    denom = pre_total * from_prefix + suf_total * from_suffix
    numer_all = pre_numer * from_prefix[..., None] + suf_num * from_suffix[..., None]
    context = (
        (numer_all / denom[..., None])
        .astype(jnp.bfloat16)
        .reshape(local_reqs, heads_kv * GROUP * HEAD_DIM)
    )
    partial_out = jnp.dot(
        lax.all_gather(context, "prefix", axis=0, tiled=True),
        out_weight,
        preferred_element_type=jnp.float32,
    )
    return lax.psum_scatter(partial_out, "kvhead", scatter_dimension=0, tiled=True).astype(
        jnp.bfloat16
    )


def solution(mesh):
    placed = (
        P("prefix", "kvhead"),
        P("prefix", "kvhead"),
        P("prefix", "kvhead"),
        P("prefix", None, "kvhead"),
        P("prefix", None, "kvhead"),
        P(),
        P("prefix"),
        P("kvhead", "prefix"),
    )
    return jax.shard_map(
        on_device, mesh=mesh, in_specs=placed, out_specs=P("kvhead", "prefix"), check_vma=False
    )
```

profile of v0, /device:TPU:1, one launch (start us, length us, event | category | flops | bytes accessed | tf_op | source)
XLA Modules:
  0.0 548.1 jit_solution(2237365967220073280)
XLA Ops:
  6.5 0.0 copy-start
  6.5 0.0 reduce-scatter.4.cloned.1.call-start
  6.5 41.5 %all_gather.6 = bf16[256,1024]{1,0:T(8,128)(2,1)S(1)} all-gather(bf16[8,1024]{1,0:T(8,128)(2,1)} %param.10), channel_id=1, replica_groups=mesh['prefix'=32,'kvhead'=8] {'prefix'}, dimensions={0}, use_global_device_ids=true | all-gather | bytes 540672 | tf_op jit(solution)/shard_map/all_gather | solution.py:29
  48.1 0.2 transpose_reshape_reshape_transpose_reshape.3
  48.3 44.9 %while.14 = (s32[]{:T(128)}, f32[4,1,512]{2,1,0:T(1,128)S(1)}, f32[4,1,512]{2,1,0:T(1,128)S(1)}, bf16[4,1,512,128]{3,2,1,0:T(8,128)(2,1)}, bf16[4,1,512,128]{3,2...) while((s32[]{:T(128)}, f32[4,1,512]{2,1,0:T(1,128)S(1)}, ...), condition=%wide.region_3.4_spmd, body=%wide.region_0.3_spmd.sunk | while | flops 2176973824 | bytes 63193220 | solution.py:54
  48.3 4.0 multiply_reduce_fusion.2
  52.3 4.2 convert_reduce_fusion.3
  56.5 0.0 copy-done.2
  56.5 3.0 fusion.44
  59.5 4.0 multiply_reduce_fusion.2
  63.5 0.0 copy-start.2
  63.5 4.2 convert_reduce_fusion.3
  67.7 0.0 copy-done.2
  67.7 3.0 fusion.44
  70.7 4.0 multiply_reduce_fusion.2
  74.8 0.0 copy-start.2
  74.8 4.2 convert_reduce_fusion.3
  78.9 0.0 copy-done.2
  78.9 3.0 fusion.44
  82.0 4.0 multiply_reduce_fusion.2
  86.0 0.0 copy-start.2
  86.0 4.2 convert_reduce_fusion.3
  90.2 0.0 copy-done.2
  90.2 3.0 fusion.44
  93.2 1.3 reshape.128
  94.5 0.7 transpose_reshape_transpose.8
  95.2 0.1 transpose_reshape_transpose.7
  95.4 112.5 %pmax.7 = f32[256,1,8]{2,0,1:T(8,128)S(1)} all-reduce(f32[256,1,8]{2,0,1:T(8,128)S(1)} %transpose_reshape_transpose.7), channel_id=1, replica_groups=mesh['prefix'=32,'kvhead'=8] {'prefix'}, use_global_device_ids=true, to_apply=%region_4.5 | all-reduce | flops 2048 | bytes 16384 | tf_op jit(solution)/shard_map/pmax | solution.py:63
  207.8 0.9 exponential_multiply_fusion
  208.8 0.3 mul.62
  209.1 1.3 bitcast_multiply_fusion
  210.4 0.0 reduce-scatter.4.cloned.1.call-update
  210.4 0.0 reduce-scatter.6.cloned.1.call-start
  210.5 1.3 dynamic-slice
  212.4 110.6 %all-reduce = f32[256,1,8]{2,0,1:T(8,128)S(1)} all-reduce(f32[256,1,8]{2,0,1:T(8,128)S(1)} %exponential_multiply_fusion), channel_id=3, replica_groups=mesh['prefix'=32,'kvhead'=8] {'prefix'}, use_global_device_ids=true, to_apply=%region_8.9.clone | all-reduce | flops 2048 | bytes 16384
  323.0 0.9 select_reduce_fusion
  323.8 0.1 iota_compare_fusion
  323.9 0.0 copy-done
  323.9 0.0 copy-done.1
  323.9 0.7 fusion.32
  324.6 0.2 convert_reduce_fusion.1
  324.9 128.1 %reduce-scatter.4.cloned.1.call-done = f32[8,1024]{1,0:T(8,128)} async-done(((f32[256,1024]{1,0:T(8,128)}), f32[8,1024]{1,0:T(8,128)}) %reduce-scatter.4.cloned.1.call-update) | async-done | bytes 32784 | tf_op jit(solution)/shard_map/reduce_scatter | solution.py:69
  453.0 2.0 fusion.23
  455.0 35.8 %all_gather.7 = bf16[256,1024]{1,0:T(8,128)(2,1)S(1)} all-gather(bf16[8,1024]{1,0:T(8,128)(2,1)S(1)} %bitcast.95), channel_id=1, replica_groups=mesh['prefix'=32,'kvhead'=8] {'prefix'}, dimensions={0}, use_global_device_ids=true | all-gather | bytes 540672 | tf_op jit(solution)/shard_map/all_gather | solution.py:104
  490.8 2.0 fusion.33
  492.9 0.0 reduce-scatter.6.cloned.1.call-update
  492.9 47.0 %reduce-scatter.6.cloned.1.call-done = f32[32,256]{1,0:T(8,128)} async-done(((f32[256,256]{1,0:T(8,128)}), f32[32,256]{1,0:T(8,128)}) %reduce-scatter.6.cloned.1.call-update) | async-done | bytes 32784 | tf_op jit(solution)/shard_map/reduce_scatter | solution.py:108
  539.9 1.4 convert_element_type.41
  (13 shorter events, 0.2 us)
Async XLA Ops:
  6.5 317.4 %copy-start = (bf16[8,1024,128]{2,1,0:T(8,128)(2,1)S(1)}, bf16[8,1024,128]{2,1,0:T(8,128)(2,1)}, u32[]{:S(2)}) copy-start(bf16[8,1024,128]{2,1,0:T(8,128)(2,1)} %param.13) | copy-start | bytes 6291460
  6.5 446.5 %reduce-scatter.4.cloned.1.call-start = ((), (), s32[]{:S(2)}) async-start(), calls=%async_computation.2 | async-start | bytes 1081344 | tf_op jit(solution)/shard_map/reduce_scatter | solution.py:69
  52.3 4.2 copy-start.2
  63.5 4.2 copy-start.2
  74.8 4.2 copy-start.2
  86.0 4.2 copy-start.2
  93.2 230.7 %copy-start.1 = (bf16[8,1024]{1,0:T(8,128)(2,1)S(1)}, bf16[8,1024]{1,0:T(8,128)(2,1)}, u32[]{:S(2)}) copy-start(bf16[8,1024]{1,0:T(8,128)(2,1)} %param.10) | copy-start | bytes 49156
  210.4 329.5 %reduce-scatter.6.cloned.1.call-start = ((), (), s32[]{:S(2)}) async-start(), calls=%async_computation.3 | async-start | bytes 294912 | tf_op jit(solution)/shard_map/reduce_scatter | solution.py:108
Sparse Core Ops, SparseCore 0:
  210.5 242.4 reduce-scatter.3
  493.0 46.8 reduce-scatter.5
where the time goes:
time: 550 us; the launch traced here: 548 us
  blocking collectives  300 us (55%)
  waiting for transfers between devices  175 us (32%)
  matrix products  32.9 us (6%)
  other arithmetic  21.4 us (4%)
  between operations  14.1 us (3%)
    reduce_scatter x1, waiting for transfers between devices, on_device(): lax.psum_scatter(scaled, 'prefix', scatter_dimension=0, tiled=True)  128 us
    pmax x1, blocking collectives, on_device(): top_all = lax.pmax(peak, 'prefix')  112 us
    unnamed x1, blocking collectives  111 us
    reduce_scatter x1, waiting for transfers between devices, on_device(): lax.psum_scatter(partial_out, 'kvhead', scatter_dimension=0, tiled=True)  47 us
    all_gather x1, blocking collectives, on_device(): everyone = lax.all_gather(queries, 'prefix', axis=0, tiled=True)  41.5 us
    all_gather x1, blocking collectives, on_device(): lax.all_gather(context, 'prefix', axis=0, tiled=True)  35.8 us
    reduce_sum x4, other arithmetic, segment_part(): total = jnp.sum(probs, axis=-1, dtype=jnp.float32)  16.6 us
    dot_general x4, matrix products, segment_part(): jnp.einsum('gre,sge->grs', q_block, keys, preferred_element_type=jnp.floa...  16 us
  transfers between devices with their start and end apart: 2, of which 2 were waited for; matrix products, arithmetic and copies ran while one was open for 1% of the time, Pallas kernels for 0%

commit v1 on v0

v1 whole, which is shorter than its diff:
```python
import functools
import math

import jax
import jax.numpy as jnp
from jax import lax
from jax.experimental import pallas as pl
from jax.experimental.pallas import tpu as pltpu
from jax.sharding import Mesh
from jax.sharding import PartitionSpec as P

HEAD_DIM = 128
GROUP = 8
WIDTH = GROUP * HEAD_DIM
PACKED = WIDTH + HEAD_DIM
SCALE2 = HEAD_DIM ** (-0.5) * math.log2(math.e)
CONTRACT_LAST = (((1,), (1,)), ((), ()))
VMEM_BYTES = 56 << 20


def split3(x):
    high = x.astype(jnp.bfloat16).astype(jnp.float32)
    rest = x - high
    mid = rest.astype(jnp.bfloat16).astype(jnp.float32)
    return high, mid, rest - mid


def store_scaled_rows(q_ref, rows_ref, slots):
    for g in range(GROUP):
        q = q_ref[:, g * HEAD_DIM : (g + 1) * HEAD_DIM].astype(jnp.float32) * SCALE2
        high = q.astype(jnp.bfloat16)
        low = (q - high.astype(jnp.float32)).astype(jnp.bfloat16)
        rows_ref[g * slots : (g + 1) * slots, :HEAD_DIM] = high
        rows_ref[g * slots : (g + 1) * slots, HEAD_DIM:] = low


def prefix_kernel(
    q_ref, k_hbm, v_hbm, out_ref, rows, keys, values, acc, peak, sems, *, slots, step, block
):
    count = k_hbm.shape[0] // step
    copies = []
    for j in range(count):
        part = pl.ds(j * step, step)
        copies.append(
            (
                pltpu.make_async_copy(k_hbm.at[part], keys.at[part], sems.at[0, j]),
                pltpu.make_async_copy(v_hbm.at[part], values.at[part], sems.at[1, j]),
            )
        )
    for pair in copies:
        for copy in pair:
            copy.start()
    store_scaled_rows(q_ref, rows, slots)
    total_rows = GROUP * slots

    def operands(part):
        k = keys[part, :]
        v = values[part, :]
        return (
            jnp.concatenate([k, k], axis=1),
            jnp.concatenate([v, jnp.ones_like(v)], axis=1),
        )

    for j in range(count):
        for copy in copies[j]:
            copy.wait()
        k2, v1 = operands(pl.ds(j * step, step))
        for r in range(0, total_rows, block):
            scores = lax.dot_general(
                rows[r : r + block, :], k2, CONTRACT_LAST, preferred_element_type=jnp.float32
            )
            probs = jnp.exp2(scores).astype(jnp.bfloat16)
            part = jnp.dot(probs, v1, preferred_element_type=jnp.float32)
            if j == 0:
                acc[r : r + block, :] = part
            else:
                acc[r : r + block, :] += part
    peak[...] = jnp.zeros_like(peak)
    sums = acc[:, HEAD_DIM:]
    fine = (sums >= 1e-25) & (sums <= 1e30)
    bad = jnp.max(jnp.where(fine, 0.0, 1.0))

    @pl.when(bad > 0.0)
    def _():
        peak[...] = jnp.full_like(peak, -1e38)
        acc[...] = jnp.zeros_like(acc)
        small = 512

        def body(i, carry):
            k2, v1 = operands(pl.ds(pl.multiple_of(i * small, small), small))

            def rows_body(r, inner):
                here = pl.ds(pl.multiple_of(r * block, block), block)
                scores = lax.dot_general(
                    rows[here, :], k2, CONTRACT_LAST, preferred_element_type=jnp.float32
                )
                old = peak[here, :]
                new = jnp.maximum(old, jnp.max(scores, axis=1, keepdims=True))
                probs = jnp.exp2(scores - new[:, :1]).astype(jnp.bfloat16)
                decay = jnp.exp2(old[:, :1] - new[:, :1])
                acc[here, :] = acc[here, :] * decay + jnp.dot(
                    probs, v1, preferred_element_type=jnp.float32
                )
                peak[here, :] = new
                return inner

            return lax.fori_loop(0, total_rows // block, rows_body, carry)

        lax.fori_loop(0, k_hbm.shape[0] // small, body, 0)

    lane = lax.broadcasted_iota(jnp.int32, (slots, HEAD_DIM), 1)
    stats = jnp.zeros((slots, HEAD_DIM), jnp.float32)
    for g in range(GROUP):
        here = slice(g * slots, (g + 1) * slots)
        sums = acc[here, HEAD_DIM:]
        out_ref[:, g * HEAD_DIM : (g + 1) * HEAD_DIM] = (
            acc[here, :HEAD_DIM] / sums
        ).astype(jnp.bfloat16)
        for i, piece in enumerate(split3(peak[here, :] + jnp.log2(sums))):
            stats = jnp.where(lane == i * GROUP + g, piece, stats)
    out_ref[:, WIDTH:] = stats.astype(jnp.bfloat16)


def prefix_part(queries, keys, values, step=2048, block=256):
    slots = queries.shape[0]
    length = keys.shape[0]
    rows = GROUP * slots
    return pl.pallas_call(
        functools.partial(prefix_kernel, slots=slots, step=step, block=block),
        in_specs=[
            pl.BlockSpec(memory_space=pltpu.VMEM),
            pl.BlockSpec(memory_space=pl.ANY),
            pl.BlockSpec(memory_space=pl.ANY),
        ],
        out_specs=pl.BlockSpec(memory_space=pltpu.VMEM),
        out_shape=jax.ShapeDtypeStruct((slots, PACKED), jnp.bfloat16),
        scratch_shapes=[
            pltpu.VMEM((rows, 2 * HEAD_DIM), jnp.bfloat16),
            pltpu.VMEM((length, HEAD_DIM), jnp.bfloat16),
            pltpu.VMEM((length, HEAD_DIM), jnp.bfloat16),
            pltpu.VMEM((rows, 2 * HEAD_DIM), jnp.float32),
            pltpu.VMEM((rows, HEAD_DIM), jnp.float32),
            pltpu.SemaphoreType.DMA((2, length // step)),
        ],
        compiler_params=pltpu.CompilerParams(vmem_limit_bytes=VMEM_BYTES),
        name="prefix_part",
    )(queries, keys, values)


def suffix_kernel(
    request_ref, lengths_ref, q_ref, k_hbm, v_hbm, ctx_ref, lse_ref, keys, values, sems
):
    slots, span = k_hbm.shape[0], k_hbm.shape[1]
    rows = GROUP * slots
    key_copies = [pltpu.make_async_copy(k_hbm.at[b], keys.at[b], sems.at[0, b]) for b in range(slots)]
    value_copies = [
        pltpu.make_async_copy(v_hbm.at[b], values.at[b], sems.at[1, b]) for b in range(slots)
    ]
    for copy in key_copies + value_copies:
        copy.start()
    q = jnp.concatenate(
        [q_ref[:, g * HEAD_DIM : (g + 1) * HEAD_DIM].astype(jnp.float32) for g in range(GROUP)],
        axis=0,
    ).astype(jnp.bfloat16)
    slot = lax.rem(lax.broadcasted_iota(jnp.int32, (rows, span), 0), slots)
    limit = jnp.zeros((rows, span), jnp.int32)
    for b in range(slots):
        limit = jnp.where(slot == b, lengths_ref[request_ref[b]], limit)
    live = lax.broadcasted_iota(jnp.int32, (rows, span), 1) < limit
    scores = jnp.zeros((rows, span), jnp.float32)
    for b in range(slots):
        key_copies[b].wait()
        mine = lax.dot_general(q, keys[b], CONTRACT_LAST, preferred_element_type=jnp.float32)
        scores = jnp.where(slot == b, mine, scores)
    scores = jnp.where(live, scores * SCALE2, -1e30)
    top = jnp.max(scores, axis=1, keepdims=True)
    probs = jnp.where(live, jnp.exp2(scores - top), 0.0).astype(jnp.bfloat16).astype(jnp.float32)
    total = jnp.sum(probs, axis=1, keepdims=True)
    numer = jnp.zeros((rows, HEAD_DIM), jnp.float32)
    for b in range(slots):
        value_copies[b].wait()
        mine = jnp.where(slot == b, probs, 0.0).astype(jnp.bfloat16)
        numer += jnp.dot(mine, values[b], preferred_element_type=jnp.float32)
    ctx = numer / total
    lse = jnp.broadcast_to(top + jnp.log2(total), (rows, HEAD_DIM))
    for g in range(GROUP):
        here = slice(g * slots, (g + 1) * slots)
        ctx_ref[:, g * HEAD_DIM : (g + 1) * HEAD_DIM] = ctx[here]
        lse_ref[:, g * HEAD_DIM : (g + 1) * HEAD_DIM] = lse[here]


def suffix_part(queries, keys, values, lengths, request):
    slots, span, _ = keys.shape
    vmem = pl.BlockSpec(memory_space=pltpu.VMEM)
    smem = pl.BlockSpec(memory_space=pltpu.SMEM)
    anywhere = pl.BlockSpec(memory_space=pl.ANY)
    return pl.pallas_call(
        suffix_kernel,
        in_specs=[smem, smem, vmem, anywhere, anywhere],
        out_specs=[vmem, vmem],
        out_shape=[jax.ShapeDtypeStruct((slots, WIDTH), jnp.float32)] * 2,
        scratch_shapes=[
            pltpu.VMEM((slots, span, HEAD_DIM), jnp.bfloat16),
            pltpu.VMEM((slots, span, HEAD_DIM), jnp.bfloat16),
            pltpu.SemaphoreType.DMA((2, slots)),
        ],
        compiler_params=pltpu.CompilerParams(vmem_limit_bytes=VMEM_BYTES),
        name="suffix_part",
    )(request, lengths, queries, keys, values)


def spread_lse(stats):
    source = lax.broadcasted_iota(jnp.int32, (HEAD_DIM, WIDTH), 0)
    head = lax.broadcasted_iota(jnp.int32, (HEAD_DIM, WIDTH), 1) // HEAD_DIM
    chosen = (lax.rem(source, GROUP) == head) & (source < 3 * GROUP)
    chosen = jnp.where(chosen, 1.0, 0.0).astype(jnp.bfloat16)
    return jnp.dot(stats, chosen, preferred_element_type=jnp.float32)


def merge_kernel(parts_ref, ctx_ref, lse_ref, out_ref, *, sources):
    slots = ctx_ref.shape[0]
    copies = out_ref.shape[0] // slots
    lse = spread_lse(parts_ref[:, WIDTH:])
    lse = [lse[i * slots : (i + 1) * slots] for i in range(sources)]
    top = functools.reduce(jnp.maximum, lse, lse_ref[...])
    weight = jnp.exp2(lse_ref[...] - top)
    total, numer = weight, weight * ctx_ref[...]
    parts = parts_ref[:, :WIDTH].astype(jnp.float32)
    for i in range(sources):
        weight = jnp.exp2(lse[i] - top)
        total += weight
        numer += weight * parts[i * slots : (i + 1) * slots]
    context = numer / total
    out_ref[...] = jnp.concatenate([context] * copies, axis=0).astype(jnp.bfloat16)


def merge(parts, ctx, lse, copies):
    slots = ctx.shape[0]
    return pl.pallas_call(
        functools.partial(merge_kernel, sources=parts.shape[0] // slots),
        out_shape=jax.ShapeDtypeStruct((copies * slots, WIDTH), jnp.bfloat16),
        compiler_params=pltpu.CompilerParams(vmem_limit_bytes=VMEM_BYTES),
        name="merge",
    )(parts, ctx, lse)


def on_device(
    queries,
    prefix_keys,
    prefix_values,
    suffix_keys,
    suffix_values,
    suffix_lengths,
    slot_request,
    out_weight,
):
    owners = lax.axis_size("prefix")
    swap = functools.partial(lax.all_to_all, axis_name="prefix", split_axis=0, concat_axis=0, tiled=True)
    everyone = swap(jnp.tile(queries, (owners, 1)))
    suffix_ctx, suffix_lse = suffix_part(
        queries, suffix_keys, suffix_values, suffix_lengths, slot_request
    )
    parts = swap(prefix_part(everyone, prefix_keys, prefix_values))
    context = swap(merge(parts, suffix_ctx, suffix_lse, owners))
    partial_out = jnp.dot(context, out_weight, preferred_element_type=jnp.float32)
    heads = lax.axis_size("kvhead")
    batch = partial_out.shape[0]
    pieces = lax.all_to_all(
        partial_out.astype(jnp.bfloat16), "kvhead", split_axis=0, concat_axis=0, tiled=True
    )
    pieces = pieces.reshape(heads, batch // heads, -1).astype(jnp.float32)
    return jnp.sum(pieces, axis=0).astype(jnp.bfloat16)


def solution(mesh):
    placed = (
        P("prefix", "kvhead"),
        P("prefix", "kvhead"),
        P("prefix", "kvhead"),
        P("prefix", None, "kvhead"),
        P("prefix", None, "kvhead"),
        P(),
        P("prefix"),
        P("kvhead", "prefix"),
    )
    return jax.shard_map(
        on_device, mesh=mesh, in_specs=placed, out_specs=P("kvhead", "prefix"), check_vma=False
    )
```

time: 550 us -> 207 us (0.38)
  blocking collectives: 300 us -> 61.7 us
  waiting for transfers between devices: 175 us -> 9.38 us
  Pallas kernels: 0 us -> 125 us
  matrix products: 32.9 us -> 0.3 us
  other arithmetic: 21.4 us -> 0.63 us
  between operations: 14.1 us -> 0.04 us
  starting transfers between devices: 0.04 us -> 7.5 us
    reduce_scatter x2 -> x0, waiting for transfers between devices: 175 us -> none  [the longest x1 128 us: on_device(): lax.psum_scatter(scaled, 'prefix', scatter_dimension=0, tiled=True)]
    pallas_call x0 -> x3, Pallas kernels: none -> 125 us  [the longest x1 117 us: prefix_part(): pl.pallas_call(functools.partial(prefix_kernel, slots=slots, step=step, b...]
    pmax x1 -> x0, blocking collectives: 112 us -> none  [on_device(): top_all = lax.pmax(peak, 'prefix')]
    unnamed x1 -> x0, blocking collectives: 111 us -> none
    all_gather x2 -> x0, blocking collectives: 77.3 us -> none  [the longest x1 41.5 us: on_device(): everyone = lax.all_gather(queries, 'prefix', axis=0, tiled=True)]
    all_to_all x0 -> x3, blocking collectives: none -> 61.7 us  [the longest x1 26.1 us: on_device(): everyone = swap(jnp.tile(queries, (owners, 1)))]
    dot_general x11 -> x1, matrix products: 32.9 us -> 0.3 us  [on_device(): jnp.dot(context, out_weight, preferred_element_type=jnp.float32)]
    reduce_sum x6 -> x1, other arithmetic: 17.7 us -> 0.63 us  [on_device(): return jnp.sum(pieces, axis=0).astype(jnp.bfloat16)]
  transfers between devices with their start and end apart: 2 -> 1, of which waited for: 2 -> 1; matrix products, arithmetic and copies ran while one was open for 1% -> 0% of each run, Pallas kernels for 0% -> 3%
where the time goes in v1:
time: 207 us
  Pallas kernels  125 us (60%)
  blocking collectives  61.7 us (30%)
  waiting for transfers between devices  9.38 us (5%)
  starting transfers between devices  7.5 us (4%)
    pallas_call x1, Pallas kernels, prefix_part(): pl.pallas_call(functools.partial(prefix_kernel, slots=slots, step=step, b...  117 us
    all_to_all x1, blocking collectives, on_device(): everyone = swap(jnp.tile(queries, (owners, 1)))  26.1 us
    all_to_all x1, blocking collectives, on_device(): context = swap(merge(parts, suffix_ctx, suffix_lse, owners))  20.8 us
    all_to_all x1, blocking collectives, on_device(): lax.all_to_all(partial_out.astype(jnp.bfloat16), 'kvhead', split_axis=0,...  14.8 us
    all_to_all x1, waiting for transfers between devices, on_device(): parts = swap(prefix_part(everyone, prefix_keys, prefix_values))  9.38 us
    all_to_all x1, starting transfers between devices, on_device(): parts = swap(prefix_part(everyone, prefix_keys, prefix_values))  7.5 us
    pallas_call x1, Pallas kernels, suffix_part(): pl.pallas_call(suffix_kernel, in_specs=[smem, smem, vmem, anywhere, anywh...  5.66 us
  transfers between devices with their start and end apart: 1, of which 1 were waited for; matrix products, arithmetic and copies ran while one was open for 0% of the time, Pallas kernels for 3%

profile of v1, /device:TPU:1, one launch (start us, length us, event | category | flops | bytes accessed | tf_op | source)
XLA Modules:
  0.0 206.7 jit_solution(7612362173806590671)
XLA Ops:
  0.0 0.0 copy-start
  0.0 0.8 tile.2
  0.8 26.1 %all_to_all.40 = bf16[32,8,1024]{2,1,0:T(8,128)(2,1)} all-to-all(bf16[32,8,1024]{2,1,0:T(8,128)(2,1)S(1)} %tile.2), channel_id=1, replica_groups=mesh['prefix'=32,'kvhead'=8] {'prefix'}, dimensions={0} | all-to-all | bytes 1048576 | tf_op jit(solution)/shard_map/all_to_all | solution.py:259
  26.9 117.4 %prefix_part.1 = bf16[256,1152]{1,0:T(8,128)(2,1)} custom-call(bf16[256,1024]{1,0:T(8,128)(2,1)} %bitcast.12, bf16[8192,128]{1,0:T(8,128)(2,1)} %k_hbm.2, bf16[8192,128]{1,0:T(8,128)(2,1)} %v_hbm.2), custom_call_target="tpu_custom_call" | custom-call | tf_op jit(solution)/shard_map/prefix_part/pallas_call | solution.py:128
  144.4 7.5 %all-to-all-start.1 = ((bf16[32,8,1152]{2,1,0:T(8,128)(2,1)}), bf16[32,8,1152]{2,1,0:T(8,128)(2,1)S(1)}, u32[]{:S(2)}, u32[]{:S(2)}) async-start(bf16[32,8,1152]{2,1,0:T(8,128)(2,1)} %bitcast.10), calls=%async_computation.1 | async-start | bytes 1179648 | tf_op jit(solution)/shard_map/all_to_all | solution.py:263
  151.9 5.7 %suffix_part.1 = (f32[8,1024]{1,0:T(8,128)}, f32[8,1024]{1,0:T(8,128)}) custom-call(s32[8]{0:T(128)} %request_ref.1, s32[256]{0:T(256)} %lengths_ref.1, bf16[8,1024]{1,0:T(8,128)(2,1)} %q_ref.1, bf16[8,1024,128]{2,1,0:T(8,128)(2,1)} %k_hbm.3, bf16[8,1024,128]{2,1,0:T(8,128)(2,1)} %v_hbm.3), custom_call_target="tpu_custom_call" | custom-call | tf_op jit(solution)/shard_map/suffix_part/pallas_call | solution.py:197
  157.5 9.4 %all-to-all-done.1 = bf16[32,8,1152]{2,1,0:T(8,128)(2,1)S(1)} async-done(((bf16[32,8,1152]{2,1,0:T(8,128)(2,1)}), bf16[32,8,1152]{2,1,0:T(8,128)(2,1)S(1)}, u32[]{:S(2)}, u32[]{:S(2)}) %all-to-all-start.1) | async-done | bytes 589856 | tf_op jit(solution)/shard_map/all_to_all | solution.py:263
  166.9 0.0 copy-start.1
  166.9 0.8 copy-done.1
  167.7 2.4 %merge.1 = bf16[256,1024]{1,0:T(8,128)(2,1)} custom-call(bf16[256,1152]{1,0:T(8,128)(2,1)} %bitcast.9, f32[8,1024]{1,0:T(8,128)} %get-tuple-element.7.ctx_ref, f32[8,1024]{1,0:T(8,128)} %get-tuple-element.8.lse_ref), custom_call_target="tpu_custom_call" | custom-call | tf_op jit(solution)/shard_map/merge/pallas_call | solution.py:239
  170.1 20.8 %all_to_all.41 = bf16[32,8,1024]{2,1,0:T(8,128)(2,1)S(1)} all-to-all(bf16[32,8,1024]{2,1,0:T(8,128)(2,1)} %bitcast.11), channel_id=1, replica_groups=mesh['prefix'=32,'kvhead'=8] {'prefix'}, dimensions={0} | all-to-all | bytes 1048576 | tf_op jit(solution)/shard_map/all_to_all | solution.py:264
  191.0 0.0 copy-done
  191.0 0.3 convolution_convert_fusion
  191.3 14.8 %all_to_all.42 = bf16[8,32,256]{2,1,0:T(8,128)(2,1)S(1)} all-to-all(bf16[8,32,256]{2,1,0:T(8,128)(2,1)S(1)} %bitcast.13), channel_id=1, replica_groups=mesh['prefix'=32,'kvhead'=8] {'kvhead'}, dimensions={0} | all-to-all | bytes 262144 | tf_op jit(solution)/shard_map/all_to_all | solution.py:268
  206.1 0.6 reduce_sum.12
Async XLA Ops:
  0.0 191.0 %copy-start = (bf16[1024,256]{1,0:T(8,128)(2,1)S(1)}, bf16[1024,256]{1,0:T(8,128)(2,1)}, u32[]{:S(2)}) copy-start(bf16[1024,256]{1,0:T(8,128)(2,1)} %param.15) | copy-start | bytes 1572868
  144.4 22.6 %all-to-all-start.1 = ((bf16[32,8,1152]{2,1,0:T(8,128)(2,1)}), bf16[32,8,1152]{2,1,0:T(8,128)(2,1)S(1)}, u32[]{:S(2)}, u32[]{:S(2)}) async-start(bf16[32,8,1152]{2,1,0:T(8,128)(2,1)} %bitcast.10), calls=%async_computation.1 | async-start | bytes 1179648 | tf_op jit(solution)/shard_map/all_to_all | solution.py:263
  166.9 0.8 copy-start.1

commit v2 on v1

v2 whole, which is shorter than its diff:
```python
import functools
import math

import jax
import jax.numpy as jnp
from jax import lax
from jax.experimental import pallas as pl
from jax.experimental.pallas import tpu as pltpu
from jax.sharding import Mesh
from jax.sharding import PartitionSpec as P

HEAD_DIM = 128
GROUP = 8
WIDTH = GROUP * HEAD_DIM
PACKED = WIDTH + HEAD_DIM
SCALE2 = HEAD_DIM ** (-0.5) * math.log2(math.e)
CONTRACT_LAST = (((1,), (1,)), ((), ()))
PREFIX_VMEM = 24 << 20
SUFFIX_VMEM = 12 << 20
MERGE_VMEM = 12 << 20


def split3(x):
    high = x.astype(jnp.bfloat16).astype(jnp.float32)
    rest = x - high
    mid = rest.astype(jnp.bfloat16).astype(jnp.float32)
    return high, mid, rest - mid


def operands(k, v):
    return jnp.concatenate([k, k], axis=1), jnp.concatenate([v, jnp.ones_like(v)], axis=1)


def put_queries(rows, base, blocks):
    q = jnp.concatenate([block.astype(jnp.float32) for block in blocks], axis=0) * SCALE2
    slots = q.shape[0]
    for g in range(GROUP):
        here = slice(base + g * slots, base + (g + 1) * slots)
        mine = q[:, g * HEAD_DIM : (g + 1) * HEAD_DIM]
        high = mine.astype(jnp.bfloat16)
        rows[here, :HEAD_DIM] = high
        rows[here, HEAD_DIM:] = (mine - high.astype(jnp.float32)).astype(jnp.bfloat16)


def attend(rows, k_ref, v_ref, acc, peak, step, block):
    total_rows = rows.shape[0]
    length = k_ref.shape[0]
    for j in range(0, length, step):
        k2, v1 = operands(k_ref[j : j + step, :], v_ref[j : j + step, :])
        for r in range(0, total_rows, block):
            scores = lax.dot_general(
                rows[r : r + block, :], k2, CONTRACT_LAST, preferred_element_type=jnp.float32
            )
            probs = jnp.exp2(scores).astype(jnp.bfloat16)
            part = jnp.dot(probs, v1, preferred_element_type=jnp.float32)
            if j == 0:
                acc[r : r + block, :] = part
            else:
                acc[r : r + block, :] += part
    peak[...] = jnp.zeros_like(peak)
    sums = acc[:, HEAD_DIM:]
    fine = (sums >= 1e-25) & (sums <= 1e30)
    bad = jnp.max(jnp.where(fine, 0.0, 1.0))

    @pl.when(bad > 0.0)
    def _():
        peak[...] = jnp.full_like(peak, -1e38)
        acc[...] = jnp.zeros_like(acc)
        small, few = 512, 128

        def body(i, carry):
            part = pl.ds(pl.multiple_of(i * small, small), small)
            k2, v1 = operands(k_ref[part, :], v_ref[part, :])

            def rows_body(r, inner):
                here = pl.ds(pl.multiple_of(r * few, few), few)
                scores = lax.dot_general(
                    rows[here, :], k2, CONTRACT_LAST, preferred_element_type=jnp.float32
                )
                old = peak[here, :]
                new = jnp.maximum(old, jnp.max(scores, axis=1, keepdims=True))
                probs = jnp.exp2(scores - new[:, :1]).astype(jnp.bfloat16)
                decay = jnp.exp2(old[:, :1] - new[:, :1])
                acc[here, :] = acc[here, :] * decay + jnp.dot(
                    probs, v1, preferred_element_type=jnp.float32
                )
                peak[here, :] = new
                return inner

            return lax.fori_loop(0, total_rows // few, rows_body, carry)

        lax.fori_loop(0, length // small, body, 0)


def packed(acc, peak, base, slots):
    lane = lax.broadcasted_iota(jnp.int32, (slots, HEAD_DIM), 1)
    stats = jnp.zeros((slots, HEAD_DIM), jnp.float32)
    pieces = []
    for g in range(GROUP):
        here = slice(base + g * slots, base + (g + 1) * slots)
        sums = acc[here, HEAD_DIM:]
        pieces.append((acc[here, :HEAD_DIM] / sums).astype(jnp.bfloat16))
        for n, piece in enumerate(split3(peak[here, :] + jnp.log2(sums))):
            stats = jnp.where(lane == n * GROUP + g, piece, stats)
    return jnp.concatenate(pieces + [stats.astype(jnp.bfloat16)], axis=1)


def first_kernel(
    q_ref, k_ref, v_ref, suffix_ctx_ref, suffix_lse_ref, out_ref, rows, acc, peak, *, step, block
):
    classes = out_ref.shape[0]
    along, held, _ = q_ref.shape
    halves = along // classes
    order = [(c, h) for c in range(classes) for h in range(halves)]
    slots = along * held
    put_queries(rows, 0, [q_ref[h * classes + c] for c, h in order])
    attend(rows, k_ref, v_ref, acc, peak, step, block)
    here_z = lax.axis_index("z")
    place = (lax.rem(here_z, classes) * halves + here_z // classes) * held
    for g in range(GROUP):
        here = pl.ds(pl.multiple_of(g * slots + place, held), held)
        lanes = slice(g * HEAD_DIM, (g + 1) * HEAD_DIM)
        sums = acc[here, HEAD_DIM:]
        prefix_lse = peak[here, :] + jnp.log2(sums)
        suffix_lse = suffix_lse_ref[:, lanes]
        top = jnp.maximum(prefix_lse, suffix_lse)
        from_prefix = jnp.exp2(prefix_lse - top)
        from_suffix = jnp.exp2(suffix_lse - top)
        both = from_prefix + from_suffix
        acc[here, :HEAD_DIM] = (
            from_prefix * (acc[here, :HEAD_DIM] / sums) + from_suffix * suffix_ctx_ref[:, lanes]
        ) / both
        acc[here, HEAD_DIM:] = jnp.ones_like(sums)
        peak[here, :] = top + jnp.log2(both)
    out = packed(acc, peak, 0, slots)
    size = halves * held
    for c in range(classes):
        out_ref[c] = out[c * size : (c + 1) * size]


def class_kernel(*refs, turns, step, block):
    *q_refs, k_ref, v_ref, first_ref = refs[: -len(turns) - 3]
    out_refs = refs[-len(turns) - 3 : -3]
    rows, acc, peak = refs[-3:]
    across = first_ref.shape[0]
    along, held, _ = q_refs[0].shape
    halves = along // across
    size = halves * held
    slots = len(q_refs) * size
    here_x = lax.axis_index("x")
    kinds = [lax.rem(here_x + turn, across) for turn in turns]
    for i, kind in enumerate(kinds):
        put_queries(
            rows,
            i * GROUP * slots,
            [q_ref[h * across + kind] for q_ref in q_refs for h in range(halves)],
        )
    attend(rows, k_ref, v_ref, acc, peak, step, block)
    for i, kind in enumerate(kinds):
        out = packed(acc, peak, i * GROUP * slots, slots)
        for n in range(len(q_refs)):
            at = lax.rem(here_x + across - n - 1, across)
            there = pl.ds(pl.multiple_of(at * size, size), size)
            out_refs[i][there, :] = out[n * size : (n + 1) * size]
        there = pl.ds(pl.multiple_of(here_x * size, size), size)
        out_refs[i][there, :] = first_ref[kind]


def prefix_call(kernel, rows, length, operand_list, out_dims, name):
    vmem = pl.BlockSpec(memory_space=pltpu.VMEM)
    return pl.pallas_call(
        kernel,
        in_specs=[vmem] * len(operand_list),
        out_specs=[vmem] * len(out_dims),
        out_shape=[jax.ShapeDtypeStruct(dims, jnp.bfloat16) for dims in out_dims],
        scratch_shapes=[
            pltpu.VMEM((rows, 2 * HEAD_DIM), jnp.bfloat16),
            pltpu.VMEM((rows, 2 * HEAD_DIM), jnp.float32),
            pltpu.VMEM((rows, HEAD_DIM), jnp.float32),
        ],
        compiler_params=pltpu.CompilerParams(vmem_limit_bytes=PREFIX_VMEM),
        cost_estimate=pl.CostEstimate(
            flops=8 * rows * length * HEAD_DIM,
            bytes_accessed=4 * length * HEAD_DIM,
            transcendentals=rows * length,
        ),
        name=name,
    )(*operand_list)


def first_part(queries, keys, values, suffix_ctx, suffix_lse, classes):
    along, held, _ = queries.shape
    return prefix_call(
        functools.partial(first_kernel, step=4096, block=256),
        GROUP * along * held,
        keys.shape[0],
        (queries, keys, values, suffix_ctx, suffix_lse),
        [(classes, along * held // classes, PACKED)],
        "first_part",
    )[0]


def class_part(queries, keys, values, first, turns):
    classes, size, _ = first.shape
    rows = GROUP * len(queries) * size
    return prefix_call(
        functools.partial(class_kernel, turns=turns, step=4096, block=rows),
        rows * len(turns),
        keys.shape[0],
        (*queries, keys, values, first),
        [(classes * size, PACKED)] * len(turns),
        "class_part",
    )


def suffix_kernel(request_ref, lengths_ref, q_ref, keys, values, ctx_ref, lse_ref):
    slots, span = keys.shape[0], keys.shape[1]
    rows = GROUP * slots
    q = jnp.concatenate(
        [q_ref[:, g * HEAD_DIM : (g + 1) * HEAD_DIM].astype(jnp.float32) for g in range(GROUP)],
        axis=0,
    ).astype(jnp.bfloat16)
    slot = lax.rem(lax.broadcasted_iota(jnp.int32, (rows, span), 0), slots)
    limit = jnp.zeros((rows, span), jnp.int32)
    for b in range(slots):
        limit = jnp.where(slot == b, lengths_ref[request_ref[b]], limit)
    live = lax.broadcasted_iota(jnp.int32, (rows, span), 1) < limit
    scores = jnp.zeros((rows, span), jnp.float32)
    for b in range(slots):
        mine = lax.dot_general(q, keys[b], CONTRACT_LAST, preferred_element_type=jnp.float32)
        scores = jnp.where(slot == b, mine, scores)
    scores = jnp.where(live, scores * SCALE2, -1e30)
    top = jnp.max(scores, axis=1, keepdims=True)
    probs = jnp.where(live, jnp.exp2(scores - top), 0.0).astype(jnp.bfloat16).astype(jnp.float32)
    total = jnp.sum(probs, axis=1, keepdims=True)
    numer = jnp.zeros((rows, HEAD_DIM), jnp.float32)
    for b in range(slots):
        mine = jnp.where(slot == b, probs, 0.0).astype(jnp.bfloat16)
        numer += jnp.dot(mine, values[b], preferred_element_type=jnp.float32)
    ctx = numer / total
    lse = jnp.broadcast_to(top + jnp.log2(total), (rows, HEAD_DIM))
    for g in range(GROUP):
        here = slice(g * slots, (g + 1) * slots)
        ctx_ref[:, g * HEAD_DIM : (g + 1) * HEAD_DIM] = ctx[here]
        lse_ref[:, g * HEAD_DIM : (g + 1) * HEAD_DIM] = lse[here]


def suffix_part(queries, keys, values, lengths, request):
    slots = keys.shape[0]
    vmem = pl.BlockSpec(memory_space=pltpu.VMEM)
    smem = pl.BlockSpec(memory_space=pltpu.SMEM)
    return pl.pallas_call(
        suffix_kernel,
        in_specs=[smem, smem, vmem, vmem, vmem],
        out_specs=[vmem, vmem],
        out_shape=[jax.ShapeDtypeStruct((slots, WIDTH), jnp.float32)] * 2,
        compiler_params=pltpu.CompilerParams(vmem_limit_bytes=SUFFIX_VMEM),
        name="suffix_part",
    )(request, lengths, queries, keys, values)


def spread_lse(stats):
    source = lax.broadcasted_iota(jnp.int32, (HEAD_DIM, WIDTH), 0)
    head = lax.broadcasted_iota(jnp.int32, (HEAD_DIM, WIDTH), 1) // HEAD_DIM
    chosen = (lax.rem(source, GROUP) == head) & (source < 3 * GROUP)
    chosen = jnp.where(chosen, 1.0, 0.0).astype(jnp.bfloat16)
    return jnp.dot(stats, chosen, preferred_element_type=jnp.float32)


def weighted(parts, lse):
    top = functools.reduce(jnp.maximum, lse)
    total, numer = 0.0, 0.0
    for part, each in zip(parts, lse, strict=True):
        weight = jnp.exp2(each - top)
        total += weight
        numer += weight * part
    return numer / total, top + jnp.log2(total)


def pack_lse(lse):
    rows = lse.shape[0]
    lane = lax.broadcasted_iota(jnp.int32, (rows, HEAD_DIM), 1)
    stats = jnp.zeros((rows, HEAD_DIM), jnp.float32)
    for g in range(GROUP):
        for n, piece in enumerate(split3(lse[:, g * HEAD_DIM : (g + 1) * HEAD_DIM])):
            stats = jnp.where(lane == n * GROUP + g, piece, stats)
    return stats.astype(jnp.bfloat16)


def merge_x_kernel(*refs):
    *part_refs, out_ref = refs
    ctx, both = weighted(
        [part[:, :WIDTH].astype(jnp.float32) for part in part_refs],
        [spread_lse(part[:, WIDTH:]) for part in part_refs],
    )
    out_ref[:, :WIDTH] = ctx.astype(jnp.bfloat16)
    out_ref[:, WIDTH:] = pack_lse(both)


def merge_x(parts):
    return pl.pallas_call(
        merge_x_kernel,
        out_shape=jax.ShapeDtypeStruct(parts[0].shape, jnp.bfloat16),
        compiler_params=pltpu.CompilerParams(vmem_limit_bytes=MERGE_VMEM),
        name="merge_x",
    )(*parts)


def merge_z_kernel(parts_ref, out_ref, *, sources):
    slots = parts_ref.shape[0] // sources
    lse = spread_lse(parts_ref[:, WIDTH:])
    parts = parts_ref[:, :WIDTH].astype(jnp.float32)
    cut = [slice(i * slots, (i + 1) * slots) for i in range(sources)]
    context, _ = weighted([parts[c] for c in cut], [lse[c] for c in cut])
    out_ref[...] = jnp.concatenate([context] * (out_ref.shape[0] // slots), axis=0).astype(jnp.bfloat16)


def merge_z(parts, sources, copies):
    return pl.pallas_call(
        functools.partial(merge_z_kernel, sources=sources),
        out_shape=jax.ShapeDtypeStruct((parts.shape[0] // sources * copies, WIDTH), jnp.bfloat16),
        compiler_params=pltpu.CompilerParams(vmem_limit_bytes=MERGE_VMEM),
        name="merge_z",
    )(parts)


def project_kernel(context_ref, weight_ref, out_ref):
    blocks, size, _ = out_ref.shape
    product = jnp.dot(context_ref[...], weight_ref[...], preferred_element_type=jnp.float32)
    held = 8
    for b in range(blocks):
        mine = [
            product[(c * blocks + b) * held : (c * blocks + b + 1) * held]
            for c in range(size // held)
        ]
        out_ref[b] = jnp.concatenate(mine, axis=0).astype(jnp.bfloat16)


def project(context, weight, blocks):
    return pl.pallas_call(
        project_kernel,
        out_shape=jax.ShapeDtypeStruct(
            (blocks, context.shape[0] // blocks, weight.shape[1]), jnp.bfloat16
        ),
        compiler_params=pltpu.CompilerParams(vmem_limit_bytes=MERGE_VMEM),
        name="project",
    )(context, weight)


def swap(array, axes):
    return lax.all_to_all(array, axes, split_axis=0, concat_axis=0, tiled=True)


def on_device(
    queries,
    prefix_keys,
    prefix_values,
    suffix_keys,
    suffix_values,
    suffix_lengths,
    slot_request,
    out_weight,
):
    held = queries.shape[0]
    across, along, heads = lax.axis_size("x"), lax.axis_size("z"), lax.axis_size("kvhead")
    near = swap(jnp.tile(queries, (along, 1)), "z")
    near, own_queries = lax.optimization_barrier((near, queries))

    def to_other_x(array, turn):
        return lax.ppermute(array, "x", [(i, (i + turn) % across) for i in range(across)])

    turns = range(1, across)
    near = near.reshape(along, held, WIDTH)
    far = [to_other_x(near, turn) for turn in turns]
    suffix_ctx, suffix_lse = suffix_part(
        own_queries, suffix_keys, suffix_values, suffix_lengths, slot_request
    )
    first = first_part(near, prefix_keys, prefix_values, suffix_ctx, suffix_lse, across)
    first, *far = lax.optimization_barrier((first, *far))
    leaving = class_part(far, prefix_keys, prefix_values, first, tuple(turns))
    first, *leaving = lax.optimization_barrier((first, *leaving))
    arrived = [to_other_x(part, turn) for part, turn in zip(leaving, turns, strict=True)]
    staying = class_part(far, prefix_keys, prefix_values, first, (0,))
    partial = merge_x([*staying, *arrived])
    context = swap(merge_z(swap(partial, "z"), along, across * along), ("x", "z"))
    out = project(context, out_weight, heads)
    pieces = swap(out.reshape(-1, out.shape[2]), "kvhead")
    pieces = pieces.reshape(heads, across * held, -1).astype(jnp.float32)
    return jnp.sum(pieces, axis=0).astype(jnp.bfloat16)


def solution(mesh):
    x_chips = 4
    devices = mesh.devices
    split = Mesh(
        devices.reshape(x_chips, devices.shape[0] // x_chips, devices.shape[1]),
        ("x", "z", "kvhead"),
    )
    prefix = ("x", "z")
    placed = (
        P(prefix, "kvhead"),
        P(prefix, "kvhead"),
        P(prefix, "kvhead"),
        P(prefix, None, "kvhead"),
        P(prefix, None, "kvhead"),
        P(),
        P(prefix),
        P("kvhead", prefix),
    )
    return jax.shard_map(
        on_device, mesh=split, in_specs=placed, out_specs=P("kvhead", prefix), check_vma=False
    )
```

time: 207 us -> 229 us (1.11)
  Pallas kernels: 125 us -> 155 us
  waiting for transfers between devices: 9.38 us -> 0.02 us
  local copies, waits for them, and re-layouts: 1.64 us -> 6.23 us
  blocking collectives: 61.7 us -> 59.2 us
    pallas_call x3 -> x7, Pallas kernels: 125 us -> 155 us  [the longest x3 152 us: prefix_call(): pl.pallas_call(kernel, in_specs=[vmem] * len(operand_list), out_specs=[vm...]
    all_to_all x1 -> x0, waiting for transfers between devices: 9.38 us -> none  [on_device(): parts = swap(prefix_part(everyone, prefix_keys, prefix_values))]
    ppermute x0 -> x6, starting transfers between devices: none -> 7.91 us  [to_other_x(): lax.ppermute(array, 'x', [(i, (i + turn) % across) for i in range(across)])]
    all_to_all x1 -> x0, starting transfers between devices: 7.5 us -> none  [on_device(): parts = swap(prefix_part(everyone, prefix_keys, prefix_values))]
    unnamed x4 -> x16, local copies, waits for them, and re-layouts: 0.81 us -> 5.51 us
    all_to_all x3 -> x4, blocking collectives: 61.7 us -> 59.2 us  [swap(): return lax.all_to_all(array, axes, split_axis=0, concat_axis=0, tiled=True)]
  transfers between devices with their start and end apart: 1 -> 6, of which waited for: 1 -> 0; matrix products, arithmetic and copies ran while one was open for 0% -> 0% of each run, Pallas kernels for 3% -> 30%
where the time goes in v2:
time: 229 us
  Pallas kernels  155 us (68%)
  blocking collectives  59.2 us (26%)
  starting transfers between devices  7.91 us (3%)
  local copies, waits for them, and re-layouts  6.23 us (3%)
    pallas_call x3, Pallas kernels, prefix_call(): pl.pallas_call(kernel, in_specs=[vmem] * len(operand_list), out_specs=[vm...  152 us
    all_to_all x4, blocking collectives, swap(): return lax.all_to_all(array, axes, split_axis=0, concat_axis=0, tiled=True)  59.2 us
    ppermute x6, starting transfers between devices, to_other_x(): lax.ppermute(array, 'x', [(i, (i + turn) % across) for i in range(across)])  7.91 us
    unnamed x16, local copies, waits for them, and re-layouts  5.51 us
  transfers between devices with their start and end apart: 6, of which 0 were waited for; matrix products, arithmetic and copies ran while one was open for 0% of the time, Pallas kernels for 30%

profile of v2, /device:TPU:1, one launch (start us, length us, event | category | flops | bytes accessed | tf_op | source)
XLA Modules:
  0.0 229.0 jit_solution(12350038616780136194)
XLA Ops:
  0.0 0.7 tile.2
  0.7 16.6 %all_to_all.37 = bf16[8,8,1024]{2,1,0:T(8,128)(2,1)S(1)} all-to-all(bf16[8,8,1024]{2,1,0:T(8,128)(2,1)S(1)} %tile.2), channel_id=1, replica_groups=mesh['x'=4,'z'=8,'kvhead'=8] {'z'}, dimensions={0} | all-to-all | bytes 262144 | tf_op jit(solution)/shard_map/all_to_all | solution.py:351
  17.3 2.5 %collective-permute-start.2 = (bf16[8,8,1024]{2,1,0:T(8,128)(2,1)S(1)}, bf16[8,8,1024]{2,1,0:T(8,128)(2,1)S(1)}, u32[]{:S(2)}, u32[]{:S(2)}) collective-permute-start(bf16[8,8,1024]{2,1,0:T(8,128)(2,1)S(1)} %all_to_all.37), channel_id=1, source_target_pairs={{0,192},{64,0},{128,64},{192,128},{1,193},{65,1},{129,65},{193,129... | collective-permute-start | bytes 393224 | tf_op jit(solution)/shard_map/ppermute | solution.py:370
  19.8 0.5 collective-permute-start.1
  20.3 0.6 collective-permute-start
  20.9 0.0 copy-start
  20.9 1.6 copy-done
  22.5 0.0 copy-start.1
  22.5 1.6 copy-done.1
  24.1 0.0 copy-start.3
  24.1 0.7 copy-done.3
  24.8 0.0 copy-start.4
  24.8 0.7 copy-done.4
  25.5 0.0 copy-start.5
  25.5 0.7 copy-done.5
  26.2 0.0 copy-start.6
  26.2 0.0 copy-start.7
  26.2 1.9 suffix_part.1
  28.1 0.0 copy-done.6
  28.1 0.3 copy-done.7
  28.4 38.5 %first_part.1.refs_5_ = bf16[4,16,1152]{2,1,0:T(8,128)(2,1)S(1)} custom-call(bf16[8,8,1024]{2,1,0:T(8,128)(2,1)S(1)} %all_to_all.37, bf16[8192,128]{1,0:T(8,128)(2,1)S(1)} %copy-done.6, bf16[8192,128]{1,0:T(8,128)(2,1)S(1)} %copy-done.7, f32[8,1024]{1,0:T(8,128)S(1)} %get-tuple-element.22.suffix_ctx_ref, f32[8,1024]{1,0:T(8,128)S(1)} %get-tuple-element.23.suffix_lse_ref), custom_call_target="tpu_custom_call" | custom-call | flops 4294967296 | bytes 4194304 | tf_op jit(solution)/shard_map/first_part/pallas_call | solution.py:171
  66.9 0.0 collective-permute-done.2.refs_2_
  66.9 0.0 collective-permute-done.1.refs_1_
  66.9 0.0 collective-permute-done.refs_0_
  66.9 84.6 %class_part.2 = (bf16[64,1152]{1,0:T(8,128)(2,1)S(1)}, bf16[64,1152]{1,0:T(8,128)(2,1)S(1)}, bf16[64,1152]{1,0:T(8,128)(2,1)S(1)}) custom-call(bf16[8,8,1024]{2,1,0:T(8,128)(2,1)S(1)} %collective-permute-done.refs_0_, bf16[8,8,1024]{2,1,0:T(8,128)(2,1)S(1)} %collective-permute-done.1.refs_1_, bf16[8,8,1024]{2,1,0:T(8,128)(2,1)S(1)} %collective-permute-done.2.refs_2_, ...), custom_call_target="tpu_custom_call" | custom-call | flops 9663676416 | bytes 4194304 | tf_op jit(solution)/shard_map/class_part/pallas_call | solution.py:171
  151.5 1.8 collective-permute-start.3
  153.3 1.7 collective-permute-start.4
  155.1 0.8 collective-permute-start.5
  155.8 28.8 %class_part.3.refs_0_ = bf16[64,1152]{1,0:T(8,128)(2,1)S(1)} custom-call(bf16[8,8,1024]{2,1,0:T(8,128)(2,1)S(1)} %collective-permute-done.refs_0_, bf16[8,8,1024]{2,1,0:T(8,128)(2,1)S(1)} %collective-permute-done.1.refs_1_, bf16[8,8,1024]{2,1,0:T(8,128)(2,1)S(1)} %collective-permute-done.2.refs_2_, bf16[8192,128]{1,0:T(8,128)(2,1)S(1)} %copy-done.6, ...), custom_call_target="tpu_custom_call" | custom-call | flops 3221225472 | bytes 4194304 | tf_op jit(solution)/shard_map/class_part/pallas_call | solution.py:171
  184.6 0.0 copy-start.2
  184.6 0.0 collective-permute-done.3.refs_1_
  184.6 0.0 collective-permute-done.4.refs_2_
  184.6 0.0 collective-permute-done.5.refs_3_
  184.7 0.6 merge_x.1
  185.2 10.5 %all_to_all.38 = bf16[8,8,1152]{2,1,0:T(8,128)(2,1)S(1)} all-to-all(bf16[8,8,1152]{2,1,0:T(8,128)(2,1)S(1)} %bitcast.8), channel_id=1, replica_groups=mesh['x'=4,'z'=8,'kvhead'=8] {'z'}, dimensions={0} | all-to-all | bytes 294912 | tf_op jit(solution)/shard_map/all_to_all | solution.py:351
  195.7 0.2 merge_z.1
  196.0 14.5 %all_to_all.39 = bf16[32,8,1024]{2,1,0:T(8,128)(2,1)S(1)} all-to-all(bf16[32,8,1024]{2,1,0:T(8,128)(2,1)S(1)} %bitcast.6), channel_id=1, replica_groups=mesh['x'=4,'z'=8,'kvhead'=8] {'x','z'}, dimensions={0} | all-to-all | bytes 1048576 | tf_op jit(solution)/shard_map/all_to_all | solution.py:351
  210.5 0.0 copy-done.2
  210.5 0.3 project.1
  210.8 17.6 %all_to_all.40 = bf16[8,32,256]{2,1,0:T(8,128)(2,1)S(1)} all-to-all(bf16[8,32,256]{2,1,0:T(8,128)(2,1)S(1)} %project.1), channel_id=1, replica_groups=mesh['x'=4,'z'=8,'kvhead'=8] {'kvhead'}, dimensions={0} | all-to-all | bytes 262144 | tf_op jit(solution)/shard_map/all_to_all | solution.py:351
  228.4 0.6 reduce_sum.12
Async XLA Ops:
  17.3 49.6 %collective-permute-start.2 = (bf16[8,8,1024]{2,1,0:T(8,128)(2,1)S(1)}, bf16[8,8,1024]{2,1,0:T(8,128)(2,1)S(1)}, u32[]{:S(2)}, u32[]{:S(2)}) collective-permute-start(bf16[8,8,1024]{2,1,0:T(8,128)(2,1)S(1)} %all_to_all.37), channel_id=1, source_target_pairs={{0,192},{64,0},{128,64},{192,128},{1,193},{65,1},{129,65},{193,129... | collective-permute-start | bytes 393224 | tf_op jit(solution)/shard_map/ppermute | solution.py:370
  19.8 47.1 %collective-permute-start.1 = (bf16[8,8,1024]{2,1,0:T(8,128)(2,1)S(1)}, bf16[8,8,1024]{2,1,0:T(8,128)(2,1)S(1)}, u32[]{:S(2)}, u32[]{:S(2)}) collective-permute-start(bf16[8,8,1024]{2,1,0:T(8,128)(2,1)S(1)} %all_to_all.37), channel_id=1, source_target_pairs={{0,128},{64,192},{128,0},{192,64},{1,129},{65,193},{129,1},{193,65... | collective-permute-start | bytes 393224 | tf_op jit(solution)/shard_map/ppermute | solution.py:370
  20.3 46.6 %collective-permute-start = (bf16[8,8,1024]{2,1,0:T(8,128)(2,1)S(1)}, bf16[8,8,1024]{2,1,0:T(8,128)(2,1)S(1)}, u32[]{:S(2)}, u32[]{:S(2)}) collective-permute-start(bf16[8,8,1024]{2,1,0:T(8,128)(2,1)S(1)} %all_to_all.37), channel_id=1, source_target_pairs={{0,64},{64,128},{128,192},{192,0},{1,65},{65,129},{129,193},{193,1... | collective-permute-start | bytes 393224 | tf_op jit(solution)/shard_map/ppermute | solution.py:370
  20.9 1.6 copy-start
  22.5 1.6 copy-start.1
  24.1 0.7 copy-start.3
  24.8 0.7 copy-start.4
  25.5 0.7 copy-start.5
  26.2 2.0 copy-start.6
  26.2 2.2 copy-start.7
  151.5 33.1 %collective-permute-start.3 = (bf16[64,1152]{1,0:T(8,128)(2,1)S(1)}, bf16[64,1152]{1,0:T(8,128)(2,1)S(1)}, u32[]{:S(2)}, u32[]{:S(2)}) collective-permute-start(bf16[64,1152]{1,0:T(8,128)(2,1)S(1)} %get-tuple-element.32), channel_id=1, source_target_pairs={{0,64},{64,128},{128,192},{192,0},{1,65},{65,129},{129,193},{193,1... | collective-permute-start | bytes 442376 | tf_op jit(solution)/shard_map/ppermute | solution.py:370
  153.3 31.3 %collective-permute-start.4 = (bf16[64,1152]{1,0:T(8,128)(2,1)S(1)}, bf16[64,1152]{1,0:T(8,128)(2,1)S(1)}, u32[]{:S(2)}, u32[]{:S(2)}) collective-permute-start(bf16[64,1152]{1,0:T(8,128)(2,1)S(1)} %get-tuple-element.33), channel_id=1, source_target_pairs={{0,128},{64,192},{128,0},{192,64},{1,129},{65,193},{129,1},{193,65... | collective-permute-start | bytes 442376 | tf_op jit(solution)/shard_map/ppermute | solution.py:370
  155.1 29.6 %collective-permute-start.5 = (bf16[64,1152]{1,0:T(8,128)(2,1)S(1)}, bf16[64,1152]{1,0:T(8,128)(2,1)S(1)}, u32[]{:S(2)}, u32[]{:S(2)}) collective-permute-start(bf16[64,1152]{1,0:T(8,128)(2,1)S(1)} %get-tuple-element.34), channel_id=1, source_target_pairs={{0,192},{64,0},{128,64},{192,128},{1,193},{65,1},{129,65},{193,129... | collective-permute-start | bytes 442376 | tf_op jit(solution)/shard_map/ppermute | solution.py:370
  184.6 25.9 %copy-start.2 = (bf16[1024,256]{1,0:T(8,128)(2,1)S(1)}, bf16[1024,256]{1,0:T(8,128)(2,1)}, u32[]{:S(2)}) copy-start(bf16[1024,256]{1,0:T(8,128)(2,1)} %weight_ref.1) | copy-start | bytes 1572868

commit v3 on v2

--- a/solution.py
+++ b/solution.py
@@ -105,9 +105,7 @@
     return jnp.concatenate(pieces + [stats.astype(jnp.bfloat16)], axis=1)
 
 
-def first_kernel(
-    q_ref, k_ref, v_ref, suffix_ctx_ref, suffix_lse_ref, out_ref, rows, acc, peak, *, step, block
-):
+def first_kernel(q_ref, k_ref, v_ref, out_ref, rows, acc, peak, *, step, block):
     classes = out_ref.shape[0]
     along, held, _ = q_ref.shape
     halves = along // classes
@@ -115,23 +113,6 @@
     slots = along * held
     put_queries(rows, 0, [q_ref[h * classes + c] for c, h in order])
     attend(rows, k_ref, v_ref, acc, peak, step, block)
-    here_z = lax.axis_index("z")
-    place = (lax.rem(here_z, classes) * halves + here_z // classes) * held
-    for g in range(GROUP):
-        here = pl.ds(pl.multiple_of(g * slots + place, held), held)
-        lanes = slice(g * HEAD_DIM, (g + 1) * HEAD_DIM)
-        sums = acc[here, HEAD_DIM:]
-        prefix_lse = peak[here, :] + jnp.log2(sums)
-        suffix_lse = suffix_lse_ref[:, lanes]
-        top = jnp.maximum(prefix_lse, suffix_lse)
-        from_prefix = jnp.exp2(prefix_lse - top)
-        from_suffix = jnp.exp2(suffix_lse - top)
-        both = from_prefix + from_suffix
-        acc[here, :HEAD_DIM] = (
-            from_prefix * (acc[here, :HEAD_DIM] / sums) + from_suffix * suffix_ctx_ref[:, lanes]
-        ) / both
-        acc[here, HEAD_DIM:] = jnp.ones_like(sums)
-        peak[here, :] = top + jnp.log2(both)
     out = packed(acc, peak, 0, slots)
     size = halves * held
     for c in range(classes):
@@ -188,13 +169,13 @@
     )(*operand_list)
 
 
-def first_part(queries, keys, values, suffix_ctx, suffix_lse, classes):
+def first_part(queries, keys, values, classes):
     along, held, _ = queries.shape
     return prefix_call(
         functools.partial(first_kernel, step=4096, block=256),
         GROUP * along * held,
         keys.shape[0],
-        (queries, keys, values, suffix_ctx, suffix_lse),
+        (queries, keys, values),
         [(classes, along * held // classes, PACKED)],
         "first_part",
     )[0]
@@ -213,7 +194,7 @@
     )
 
 
-def suffix_kernel(request_ref, lengths_ref, q_ref, keys, values, ctx_ref, lse_ref):
+def suffix_kernel(request_ref, lengths_ref, q_ref, keys, values, first_ref, out_ref):
     slots, span = keys.shape[0], keys.shape[1]
     rows = GROUP * slots
     q = jnp.concatenate(
@@ -239,24 +220,35 @@
         numer += jnp.dot(mine, values[b], preferred_element_type=jnp.float32)
     ctx = numer / total
     lse = jnp.broadcast_to(top + jnp.log2(total), (rows, HEAD_DIM))
-    for g in range(GROUP):
-        here = slice(g * slots, (g + 1) * slots)
-        ctx_ref[:, g * HEAD_DIM : (g + 1) * HEAD_DIM] = ctx[here]
-        lse_ref[:, g * HEAD_DIM : (g + 1) * HEAD_DIM] = lse[here]
-
-
-def suffix_part(queries, keys, values, lengths, request):
-    slots = keys.shape[0]
+    classes, size, _ = first_ref.shape
+    here_z = lax.axis_index("z")
+    kind, half = lax.rem(here_z, classes), here_z // classes
+    own = lax.broadcasted_iota(jnp.int32, (size, WIDTH), 0) // slots == half
+
+    def across_lanes(array):
+        array = jnp.concatenate([array[g * slots : (g + 1) * slots] for g in range(GROUP)], axis=1)
+        return jnp.concatenate([array] * (size // slots), axis=0)
+
+    prefix = first_ref[kind]
+    prefix_ctx = prefix[:, :WIDTH].astype(jnp.float32)
+    prefix_lse = spread_lse(prefix[:, WIDTH:])
+    both_ctx, both_lse = weighted([prefix_ctx, across_lanes(ctx)], [prefix_lse, across_lanes(lse)])
+    out_ref[...] = first_ref[...]
+    out_ref[kind, :, :WIDTH] = jnp.where(own, both_ctx, prefix_ctx).astype(jnp.bfloat16)
+    out_ref[kind, :, WIDTH:] = pack_lse(jnp.where(own, both_lse, prefix_lse))
+
+
+def suffix_part(queries, keys, values, lengths, request, first):
     vmem = pl.BlockSpec(memory_space=pltpu.VMEM)
     smem = pl.BlockSpec(memory_space=pltpu.SMEM)
     return pl.pallas_call(
         suffix_kernel,
-        in_specs=[smem, smem, vmem, vmem, vmem],
-        out_specs=[vmem, vmem],
-        out_shape=[jax.ShapeDtypeStruct((slots, WIDTH), jnp.float32)] * 2,
+        in_specs=[smem, smem, vmem, vmem, vmem, vmem],
+        out_specs=vmem,
+        out_shape=jax.ShapeDtypeStruct(first.shape, jnp.bfloat16),
         compiler_params=pltpu.CompilerParams(vmem_limit_bytes=SUFFIX_VMEM),
         name="suffix_part",
-    )(request, lengths, queries, keys, values)
+    )(request, lengths, queries, keys, values, first)
 
 
 def spread_lse(stats):
@@ -322,6 +314,22 @@
         compiler_params=pltpu.CompilerParams(vmem_limit_bytes=MERGE_VMEM),
         name="merge_z",
     )(parts)
+
+
+def spread_kernel(block_ref, out_ref):
+    block = block_ref[...].astype(jnp.float32)
+    copies = out_ref.shape[0] // block.shape[0]
+    out_ref[...] = jnp.concatenate([block] * copies, axis=0).astype(out_ref.dtype)
+
+
+def spread(block, copies):
+    return pl.pallas_call(
+        spread_kernel,
+        out_shape=jax.ShapeDtypeStruct((copies * block.shape[0], block.shape[1]), block.dtype),
+        compiler_params=pltpu.CompilerParams(vmem_limit_bytes=MERGE_VMEM),
+        cost_estimate=pl.CostEstimate(flops=2 * 10**10, bytes_accessed=0, transcendentals=0),
+        name="spread",
+    )(block)
 
 
 def project_kernel(context_ref, weight_ref, out_ref):
@@ -363,19 +371,17 @@
 ):
     held = queries.shape[0]
     across, along, heads = lax.axis_size("x"), lax.axis_size("z"), lax.axis_size("kvhead")
-    near = swap(jnp.tile(queries, (along, 1)), "z")
-    near, own_queries = lax.optimization_barrier((near, queries))
-
+    near = swap(spread(queries, along), "z")
     def to_other_x(array, turn):
         return lax.ppermute(array, "x", [(i, (i + turn) % across) for i in range(across)])
 
     turns = range(1, across)
     near = near.reshape(along, held, WIDTH)
     far = [to_other_x(near, turn) for turn in turns]
-    suffix_ctx, suffix_lse = suffix_part(
-        own_queries, suffix_keys, suffix_values, suffix_lengths, slot_request
-    )
-    first = first_part(near, prefix_keys, prefix_values, suffix_ctx, suffix_lse, across)
+    first = first_part(near, prefix_keys, prefix_values, across)
+    first = suffix_part(
+        queries, suffix_keys, suffix_values, suffix_lengths, slot_request, first
+    )
     first, *far = lax.optimization_barrier((first, *far))
     leaving = class_part(far, prefix_keys, prefix_values, first, tuple(turns))
     first, *leaving = lax.optimization_barrier((first, *leaving))

time: 229 us -> 224 us (0.978)
  local copies, waits for them, and re-layouts: 6.23 us -> 0.75 us
    unnamed x16 -> x18, local copies, waits for them, and re-layouts: 5.51 us -> 0.75 us
  transfers between devices with their start and end apart: 6 -> 6, of which waited for: 0 -> 0; matrix products, arithmetic and copies ran while one was open for 0% -> 0% of each run, Pallas kernels for 30% -> 31%
where the time goes in v3:
time: 224 us
  Pallas kernels  155 us (69%)
  blocking collectives  59.4 us (27%)
  starting transfers between devices  7.77 us (3%)
    pallas_call x3, Pallas kernels, prefix_call(): pl.pallas_call(kernel, in_specs=[vmem] * len(operand_list), out_specs=[vm...  152 us
    all_to_all x4, blocking collectives, swap(): return lax.all_to_all(array, axes, split_axis=0, concat_axis=0, tiled=True)  59.4 us
    ppermute x6, starting transfers between devices, to_other_x(): lax.ppermute(array, 'x', [(i, (i + turn) % across) for i in range(across)])  7.77 us
  transfers between devices with their start and end apart: 6, of which 0 were waited for; matrix products, arithmetic and copies ran while one was open for 0% of the time, Pallas kernels for 31%

profile of v3, /device:TPU:1, one launch (start us, length us, event | category | flops | bytes accessed | tf_op | source)
XLA Modules:
  0.0 223.7 jit_solution(3704805431326675097)
XLA Ops:
  0.0 0.0 copy-start.3
  0.0 0.7 copy-done.3
  0.7 0.0 copy-start.7
  0.7 0.0 copy-start.8
  0.7 16.8 %all_to_all.37.q_ref = bf16[8,8,1024]{2,1,0:T(8,128)(2,1)S(1)} all-to-all(bf16[8,8,1024]{2,1,0:T(8,128)(2,1)S(1)} %bitcast.9), channel_id=1, replica_groups=mesh['x'=4,'z'=8,'kvhead'=8] {'z'}, dimensions={0} | all-to-all | bytes 262144 | tf_op jit(solution)/shard_map/all_to_all | solution.py:359
  17.6 0.0 copy-start
  17.6 0.0 copy-start.1
  17.6 0.0 copy-start.4
  17.6 0.0 copy-start.5
  17.6 0.0 copy-start.6
  17.6 2.6 %collective-permute-start.2 = (bf16[8,8,1024]{2,1,0:T(8,128)(2,1)S(1)}, bf16[8,8,1024]{2,1,0:T(8,128)(2,1)S(1)}, u32[]{:S(2)}, u32[]{:S(2)}) collective-permute-start(bf16[8,8,1024]{2,1,0:T(8,128)(2,1)S(1)} %all_to_all.37.q_ref), channel_id=1, source_target_pairs={{0,192},{64,0},{128,64},{192,128},{1,193},{65,1},{129,65},{193,129... | collective-permute-start | bytes 393224 | tf_op jit(solution)/shard_map/ppermute | solution.py:376
  20.2 0.5 collective-permute-start.1
  20.7 0.6 collective-permute-start
  21.3 0.0 copy-done.7
  21.3 0.0 copy-done.8
  21.3 38.3 %first_part.1.first_ref = bf16[4,16,1152]{2,1,0:T(8,128)(2,1)S(1)} custom-call(bf16[8,8,1024]{2,1,0:T(8,128)(2,1)S(1)} %all_to_all.37.q_ref, bf16[8192,128]{1,0:T(8,128)(2,1)S(1)} %copy-done.7, bf16[8192,128]{1,0:T(8,128)(2,1)S(1)} %copy-done.8), custom_call_target="tpu_custom_call" | custom-call | flops 4294967296 | bytes 4194304 | tf_op jit(solution)/shard_map/first_part/pallas_call | solution.py:152
  59.6 0.0 copy-done
  59.6 0.0 copy-done.1
  59.6 0.0 copy-done.4
  59.6 0.0 copy-done.5
  59.6 0.0 copy-done.6
  59.6 2.0 suffix_part.1.refs_5_
  61.6 0.0 collective-permute-done.2.refs_2_
  61.6 0.0 collective-permute-done.1.refs_1_
  61.6 0.0 collective-permute-done.refs_0_
  61.6 84.8 %class_part.2 = (bf16[64,1152]{1,0:T(8,128)(2,1)S(1)}, bf16[64,1152]{1,0:T(8,128)(2,1)S(1)}, bf16[64,1152]{1,0:T(8,128)(2,1)S(1)}) custom-call(bf16[8,8,1024]{2,1,0:T(8,128)(2,1)S(1)} %collective-permute-done.refs_0_, bf16[8,8,1024]{2,1,0:T(8,128)(2,1)S(1)} %collective-permute-done.1.refs_1_, bf16[8,8,1024]{2,1,0:T(8,128)(2,1)S(1)} %collective-permute-done.2.refs_2_, ...), custom_call_target="tpu_custom_call" | custom-call | flops 9663676416 | bytes 4194304 | tf_op jit(solution)/shard_map/class_part/pallas_call | solution.py:152
  146.4 1.6 collective-permute-start.3
  148.0 1.7 collective-permute-start.4
  149.8 0.8 collective-permute-start.5
  150.5 28.8 %class_part.3.refs_0_ = bf16[64,1152]{1,0:T(8,128)(2,1)S(1)} custom-call(bf16[8,8,1024]{2,1,0:T(8,128)(2,1)S(1)} %collective-permute-done.refs_0_, bf16[8,8,1024]{2,1,0:T(8,128)(2,1)S(1)} %collective-permute-done.1.refs_1_, bf16[8,8,1024]{2,1,0:T(8,128)(2,1)S(1)} %collective-permute-done.2.refs_2_, bf16[8192,128]{1,0:T(8,128)(2,1)S(1)} %copy-done.7, ...), custom_call_target="tpu_custom_call" | custom-call | flops 3221225472 | bytes 4194304 | tf_op jit(solution)/shard_map/class_part/pallas_call | solution.py:152
  179.3 0.0 copy-start.2
  179.3 0.0 collective-permute-done.3.refs_1_
  179.3 0.0 collective-permute-done.4.refs_2_
  179.3 0.0 collective-permute-done.5.refs_3_
  179.3 0.6 merge_x.1
  179.9 10.5 %all_to_all.38 = bf16[8,8,1152]{2,1,0:T(8,128)(2,1)S(1)} all-to-all(bf16[8,8,1152]{2,1,0:T(8,128)(2,1)S(1)} %bitcast.7), channel_id=1, replica_groups=mesh['x'=4,'z'=8,'kvhead'=8] {'z'}, dimensions={0} | all-to-all | bytes 294912 | tf_op jit(solution)/shard_map/all_to_all | solution.py:359
  190.4 0.2 merge_z.1
  190.7 14.5 %all_to_all.39 = bf16[32,8,1024]{2,1,0:T(8,128)(2,1)S(1)} all-to-all(bf16[32,8,1024]{2,1,0:T(8,128)(2,1)S(1)} %bitcast.5), channel_id=1, replica_groups=mesh['x'=4,'z'=8,'kvhead'=8] {'x','z'}, dimensions={0} | all-to-all | bytes 1048576 | tf_op jit(solution)/shard_map/all_to_all | solution.py:359
  205.1 0.0 copy-done.2
  205.1 0.3 project.1
  205.4 17.6 %all_to_all.40 = bf16[8,32,256]{2,1,0:T(8,128)(2,1)S(1)} all-to-all(bf16[8,32,256]{2,1,0:T(8,128)(2,1)S(1)} %project.1), channel_id=1, replica_groups=mesh['x'=4,'z'=8,'kvhead'=8] {'kvhead'}, dimensions={0} | all-to-all | bytes 262144 | tf_op jit(solution)/shard_map/all_to_all | solution.py:359
  223.1 0.6 reduce_sum.12
  (1 shorter events, 0.0 us)
Async XLA Ops:
  0.0 0.7 copy-start.3
  0.7 20.6 %copy-start.7 = (bf16[8192,128]{1,0:T(8,128)(2,1)S(1)}, bf16[8192,128]{1,0:T(8,128)(2,1)}, u32[]{:S(2)}) copy-start(bf16[8192,128]{1,0:T(8,128)(2,1)} %refs_3_.3) | copy-start | bytes 6291460
  0.7 20.6 %copy-start.8 = (bf16[8192,128]{1,0:T(8,128)(2,1)S(1)}, bf16[8192,128]{1,0:T(8,128)(2,1)}, u32[]{:S(2)}) copy-start(bf16[8192,128]{1,0:T(8,128)(2,1)} %refs_4_.3) | copy-start | bytes 6291460
  17.6 42.0 %copy-start = (bf16[8,1024,128]{2,1,0:T(8,128)(2,1)S(1)}, bf16[8,1024,128]{2,1,0:T(8,128)(2,1)}, u32[]{:S(2)}) copy-start(bf16[8,1024,128]{2,1,0:T(8,128)(2,1)} %keys.1) | copy-start | bytes 6291460
  17.6 42.0 %copy-start.1 = (bf16[8,1024,128]{2,1,0:T(8,128)(2,1)S(1)}, bf16[8,1024,128]{2,1,0:T(8,128)(2,1)}, u32[]{:S(2)}) copy-start(bf16[8,1024,128]{2,1,0:T(8,128)(2,1)} %values.1) | copy-start | bytes 6291460
  17.6 42.0 %copy-start.4 = (bf16[8,1024]{1,0:T(8,128)(2,1)S(1)}, bf16[8,1024]{1,0:T(8,128)(2,1)}, u32[]{:S(2)}) copy-start(bf16[8,1024]{1,0:T(8,128)(2,1)} %q_ref.1) | copy-start | bytes 49156
  17.6 42.0 %copy-start.5 = (s32[256]{0:T(256)S(1)}, s32[256]{0:T(256)}, u32[]{:S(2)}) copy-start(s32[256]{0:T(256)} %lengths_ref.1) | copy-start | bytes 3076
  17.6 42.0 %copy-start.6 = (s32[8]{0:T(128)S(1)}, s32[8]{0:T(128)}, u32[]{:S(2)}) copy-start(s32[8]{0:T(128)} %request_ref.1) | copy-start | bytes 100
  17.6 44.0 %collective-permute-start.2 = (bf16[8,8,1024]{2,1,0:T(8,128)(2,1)S(1)}, bf16[8,8,1024]{2,1,0:T(8,128)(2,1)S(1)}, u32[]{:S(2)}, u32[]{:S(2)}) collective-permute-start(bf16[8,8,1024]{2,1,0:T(8,128)(2,1)S(1)} %all_to_all.37.q_ref), channel_id=1, source_target_pairs={{0,192},{64,0},{128,64},{192,128},{1,193},{65,1},{129,65},{193,129... | collective-permute-start | bytes 393224 | tf_op jit(solution)/shard_map/ppermute | solution.py:376
  20.2 41.5 %collective-permute-start.1 = (bf16[8,8,1024]{2,1,0:T(8,128)(2,1)S(1)}, bf16[8,8,1024]{2,1,0:T(8,128)(2,1)S(1)}, u32[]{:S(2)}, u32[]{:S(2)}) collective-permute-start(bf16[8,8,1024]{2,1,0:T(8,128)(2,1)S(1)} %all_to_all.37.q_ref), channel_id=1, source_target_pairs={{0,128},{64,192},{128,0},{192,64},{1,129},{65,193},{129,1},{193,65... | collective-permute-start | bytes 393224 | tf_op jit(solution)/shard_map/ppermute | solution.py:376
  20.7 40.9 %collective-permute-start = (bf16[8,8,1024]{2,1,0:T(8,128)(2,1)S(1)}, bf16[8,8,1024]{2,1,0:T(8,128)(2,1)S(1)}, u32[]{:S(2)}, u32[]{:S(2)}) collective-permute-start(bf16[8,8,1024]{2,1,0:T(8,128)(2,1)S(1)} %all_to_all.37.q_ref), channel_id=1, source_target_pairs={{0,64},{64,128},{128,192},{192,0},{1,65},{65,129},{129,193},{193,1... | collective-permute-start | bytes 393224 | tf_op jit(solution)/shard_map/ppermute | solution.py:376
  146.4 32.9 %collective-permute-start.3 = (bf16[64,1152]{1,0:T(8,128)(2,1)S(1)}, bf16[64,1152]{1,0:T(8,128)(2,1)S(1)}, u32[]{:S(2)}, u32[]{:S(2)}) collective-permute-start(bf16[64,1152]{1,0:T(8,128)(2,1)S(1)} %get-tuple-element.24), channel_id=1, source_target_pairs={{0,64},{64,128},{128,192},{192,0},{1,65},{65,129},{129,193},{193,1... | collective-permute-start | bytes 442376 | tf_op jit(solution)/shard_map/ppermute | solution.py:376
  148.0 31.3 %collective-permute-start.4 = (bf16[64,1152]{1,0:T(8,128)(2,1)S(1)}, bf16[64,1152]{1,0:T(8,128)(2,1)S(1)}, u32[]{:S(2)}, u32[]{:S(2)}) collective-permute-start(bf16[64,1152]{1,0:T(8,128)(2,1)S(1)} %get-tuple-element.25), channel_id=1, source_target_pairs={{0,128},{64,192},{128,0},{192,64},{1,129},{65,193},{129,1},{193,65... | collective-permute-start | bytes 442376 | tf_op jit(solution)/shard_map/ppermute | solution.py:376
  149.8 29.6 %collective-permute-start.5 = (bf16[64,1152]{1,0:T(8,128)(2,1)S(1)}, bf16[64,1152]{1,0:T(8,128)(2,1)S(1)}, u32[]{:S(2)}, u32[]{:S(2)}) collective-permute-start(bf16[64,1152]{1,0:T(8,128)(2,1)S(1)} %get-tuple-element.26), channel_id=1, source_target_pairs={{0,192},{64,0},{128,64},{192,128},{1,193},{65,1},{129,65},{193,129... | collective-permute-start | bytes 442376 | tf_op jit(solution)/shard_map/ppermute | solution.py:376
  179.3 25.9 %copy-start.2 = (bf16[1024,256]{1,0:T(8,128)(2,1)S(1)}, bf16[1024,256]{1,0:T(8,128)(2,1)}, u32[]{:S(2)}) copy-start(bf16[1024,256]{1,0:T(8,128)(2,1)} %weight_ref.1) | copy-start | bytes 1572868

commit v4 on v3

--- a/solution.py
+++ b/solution.py
@@ -15,7 +15,8 @@
 PACKED = WIDTH + HEAD_DIM
 SCALE2 = HEAD_DIM ** (-0.5) * math.log2(math.e)
 CONTRACT_LAST = (((1,), (1,)), ((), ()))
-PREFIX_VMEM = 24 << 20
+TURNED = HEAD_DIM + 16
+PREFIX_VMEM = 32 << 20
 SUFFIX_VMEM = 12 << 20
 MERGE_VMEM = 12 << 20
 
@@ -44,8 +45,7 @@
 
 def attend(rows, k_ref, v_ref, acc, peak, step, block):
     total_rows = rows.shape[0]
-    length = k_ref.shape[0]
-    for j in range(0, length, step):
+    for j in range(0, k_ref.shape[0], step):
         k2, v1 = operands(k_ref[j : j + step, :], v_ref[j : j + step, :])
         for r in range(0, total_rows, block):
             scores = lax.dot_general(
@@ -57,6 +57,33 @@
                 acc[r : r + block, :] = part
             else:
                 acc[r : r + block, :] += part
+    check(rows, k_ref, v_ref, acc, peak)
+
+
+def attend_turned(rows, k_ref, vt_ref, acc, step):
+    turned = 0.0
+    for j in range(0, k_ref.shape[0], step):
+        k = k_ref[j : j + step, :]
+        k2 = jnp.concatenate([k, k], axis=1)
+        scores = lax.dot_general(k2, rows[...], CONTRACT_LAST, preferred_element_type=jnp.float32)
+        probs = jnp.exp2(scores).astype(jnp.bfloat16)
+        turned += jnp.dot(vt_ref[:, j : j + step], probs, preferred_element_type=jnp.float32)
+    sums = turned[HEAD_DIM : HEAD_DIM + 1]
+    acc[:, :HEAD_DIM] = jnp.transpose(turned[:HEAD_DIM] * (1.0 / sums))
+    fine = (sums >= 1e-25) & (sums <= 1e30)
+    return jnp.log2(sums), jnp.max(jnp.where(fine, 0.0, 1.0))
+
+
+def packed_turned(acc, lse, base, slots):
+    cut = [slice(base + g * slots, base + (g + 1) * slots) for g in range(GROUP)]
+    pieces = [acc[here, :HEAD_DIM].astype(jnp.bfloat16) for here in cut]
+    stats = [piece[:, here] for piece in split3(lse) for here in cut]
+    stats.append(jnp.zeros((HEAD_DIM - len(stats), slots), jnp.float32))
+    stats = jnp.transpose(jnp.concatenate(stats, axis=0))
+    return jnp.concatenate(pieces + [stats.astype(jnp.bfloat16)], axis=1)
+
+
+def check(rows, k_ref, v_ref, acc, peak):
     peak[...] = jnp.zeros_like(peak)
     sums = acc[:, HEAD_DIM:]
     fine = (sums >= 1e-25) & (sums <= 1e30)
@@ -64,32 +91,37 @@
 
     @pl.when(bad > 0.0)
     def _():
-        peak[...] = jnp.full_like(peak, -1e38)
-        acc[...] = jnp.zeros_like(acc)
-        small, few = 512, 128
-
-        def body(i, carry):
-            part = pl.ds(pl.multiple_of(i * small, small), small)
-            k2, v1 = operands(k_ref[part, :], v_ref[part, :])
-
-            def rows_body(r, inner):
-                here = pl.ds(pl.multiple_of(r * few, few), few)
-                scores = lax.dot_general(
-                    rows[here, :], k2, CONTRACT_LAST, preferred_element_type=jnp.float32
-                )
-                old = peak[here, :]
-                new = jnp.maximum(old, jnp.max(scores, axis=1, keepdims=True))
-                probs = jnp.exp2(scores - new[:, :1]).astype(jnp.bfloat16)
-                decay = jnp.exp2(old[:, :1] - new[:, :1])
-                acc[here, :] = acc[here, :] * decay + jnp.dot(
-                    probs, v1, preferred_element_type=jnp.float32
-                )
-                peak[here, :] = new
-                return inner
-
-            return lax.fori_loop(0, total_rows // few, rows_body, carry)
-
-        lax.fori_loop(0, length // small, body, 0)
+        redo(rows, k_ref, v_ref, acc, peak)
+
+
+def redo(rows, k_ref, v_ref, acc, peak):
+    total_rows, length = rows.shape[0], k_ref.shape[0]
+    peak[...] = jnp.full_like(peak, -1e38)
+    acc[...] = jnp.zeros_like(acc)
+    small, few = 512, 128
+
+    def body(i, carry):
+        part = pl.ds(pl.multiple_of(i * small, small), small)
+        k2, v1 = operands(k_ref[part, :], v_ref[part, :])
+
+        def rows_body(r, inner):
+            here = pl.ds(pl.multiple_of(r * few, few), few)
+            scores = lax.dot_general(
+                rows[here, :], k2, CONTRACT_LAST, preferred_element_type=jnp.float32
+            )
+            old = peak[here, :]
+            new = jnp.maximum(old, jnp.max(scores, axis=1, keepdims=True))
+            probs = jnp.exp2(scores - new[:, :1]).astype(jnp.bfloat16)
+            decay = jnp.exp2(old[:, :1] - new[:, :1])
+            acc[here, :] = acc[here, :] * decay + jnp.dot(
+                probs, v1, preferred_element_type=jnp.float32
+            )
+            peak[here, :] = new
+            return inner
+
+        return lax.fori_loop(0, total_rows // few, rows_body, carry)
+
+    lax.fori_loop(0, length // small, body, 0)
 
 
 def packed(acc, peak, base, slots):
@@ -105,7 +137,9 @@
     return jnp.concatenate(pieces + [stats.astype(jnp.bfloat16)], axis=1)
 
 
-def first_kernel(q_ref, k_ref, v_ref, out_ref, rows, acc, peak, *, step, block):
+def first_kernel(q_ref, k_ref, v_ref, out_ref, vt_ref, rows, acc, peak, *, step, block):
+    vt_ref[:HEAD_DIM, :] = jnp.transpose(v_ref[...])
+    vt_ref[HEAD_DIM:, :] = jnp.ones((TURNED - HEAD_DIM, v_ref.shape[0]), jnp.bfloat16)
     classes = out_ref.shape[0]
     along, held, _ = q_ref.shape
     halves = along // classes
@@ -119,8 +153,8 @@
         out_ref[c] = out[c * size : (c + 1) * size]
 
 
-def class_kernel(*refs, turns, step, block):
-    *q_refs, k_ref, v_ref, first_ref = refs[: -len(turns) - 3]
+def class_kernel(*refs, turns, step):
+    *q_refs, k_ref, v_ref, vt_ref, first_ref = refs[: -len(turns) - 3]
     out_refs = refs[-len(turns) - 3 : -3]
     rows, acc, peak = refs[-3:]
     across = first_ref.shape[0]
@@ -136,15 +170,29 @@
             i * GROUP * slots,
             [q_ref[h * across + kind] for q_ref in q_refs for h in range(halves)],
         )
-    attend(rows, k_ref, v_ref, acc, peak, step, block)
-    for i, kind in enumerate(kinds):
-        out = packed(acc, peak, i * GROUP * slots, slots)
-        for n in range(len(q_refs)):
-            at = lax.rem(here_x + across - n - 1, across)
-            there = pl.ds(pl.multiple_of(at * size, size), size)
-            out_refs[i][there, :] = out[n * size : (n + 1) * size]
-        there = pl.ds(pl.multiple_of(here_x * size, size), size)
-        out_refs[i][there, :] = first_ref[kind]
+
+    def put(outs):
+        for out, out_ref, kind in zip(outs, out_refs, kinds, strict=True):
+            for n in range(len(q_refs)):
+                at = lax.rem(here_x + across - n - 1, across)
+                there = pl.ds(pl.multiple_of(at * size, size), size)
+                out_ref[there, :] = out[n * size : (n + 1) * size]
+            there = pl.ds(pl.multiple_of(here_x * size, size), size)
+            out_ref[there, :] = first_ref[kind]
+
+    bases = [i * GROUP * slots for i in range(len(turns))]
+    if len(turns) > 1:
+        lse, bad = attend_turned(rows, k_ref, vt_ref, acc, step)
+        put([packed_turned(acc, lse, base, slots) for base in bases])
+
+        @pl.when(bad > 0.0)
+        def _():
+            redo(rows, k_ref, v_ref, acc, peak)
+            put([packed(acc, peak, base, slots) for base in bases])
+
+    else:
+        attend(rows, k_ref, v_ref, acc, peak, 2 * step, rows.shape[0])
+        put([packed(acc, peak, base, slots) for base in bases])
 
 
 def prefix_call(kernel, rows, length, operand_list, out_dims, name):
@@ -176,19 +224,19 @@
         GROUP * along * held,
         keys.shape[0],
         (queries, keys, values),
-        [(classes, along * held // classes, PACKED)],
+        [(classes, along * held // classes, PACKED), (TURNED, values.shape[0])],
         "first_part",
-    )[0]
-
-
-def class_part(queries, keys, values, first, turns):
+    )
+
+
+def class_part(queries, keys, values, turned, first, turns):
     classes, size, _ = first.shape
     rows = GROUP * len(queries) * size
     return prefix_call(
-        functools.partial(class_kernel, turns=turns, step=4096, block=rows),
+        functools.partial(class_kernel, turns=turns, step=2048),
         rows * len(turns),
         keys.shape[0],
-        (*queries, keys, values, first),
+        (*queries, keys, values, turned, first),
         [(classes * size, PACKED)] * len(turns),
         "class_part",
     )
@@ -378,15 +426,15 @@
     turns = range(1, across)
     near = near.reshape(along, held, WIDTH)
     far = [to_other_x(near, turn) for turn in turns]
-    first = first_part(near, prefix_keys, prefix_values, across)
+    first, turned = first_part(near, prefix_keys, prefix_values, across)
     first = suffix_part(
         queries, suffix_keys, suffix_values, suffix_lengths, slot_request, first
     )
     first, *far = lax.optimization_barrier((first, *far))
-    leaving = class_part(far, prefix_keys, prefix_values, first, tuple(turns))
+    leaving = class_part(far, prefix_keys, prefix_values, turned, first, tuple(turns))
     first, *leaving = lax.optimization_barrier((first, *leaving))
     arrived = [to_other_x(part, turn) for part, turn in zip(leaving, turns, strict=True)]
-    staying = class_part(far, prefix_keys, prefix_values, first, (0,))
+    staying = class_part(far, prefix_keys, prefix_values, turned, first, (0,))
     partial = merge_x([*staying, *arrived])
     context = swap(merge_z(swap(partial, "z"), along, across * along), ("x", "z"))
     out = project(context, out_weight, heads)

time: 224 us -> 223 us (level)
  no operation moved by 1% of the time
where the time goes in v4:
time: 223 us
  Pallas kernels  154 us (69%)
  blocking collectives  59.4 us (27%)
  starting transfers between devices  7.99 us (4%)
    pallas_call x3, Pallas kernels, prefix_call(): pl.pallas_call(kernel, in_specs=[vmem] * len(operand_list), out_specs=[vm...  151 us
    all_to_all x4, blocking collectives, swap(): return lax.all_to_all(array, axes, split_axis=0, concat_axis=0, tiled=True)  59.4 us
    ppermute x6, starting transfers between devices, to_other_x(): lax.ppermute(array, 'x', [(i, (i + turn) % across) for i in range(across)])  7.99 us
  transfers between devices with their start and end apart: 6, of which 0 were waited for; matrix products, arithmetic and copies ran while one was open for 0% of the time, Pallas kernels for 31%

profile of v4, /device:TPU:1, one launch (start us, length us, event | category | flops | bytes accessed | tf_op | source)
XLA Modules:
  0.0 222.8 jit_solution(770588910908749896)
XLA Ops:
  0.0 0.0 copy-start.3
  0.0 0.7 copy-done.3
  0.7 0.0 copy-start.7
  0.7 0.0 copy-start.8
  0.7 16.8 %all_to_all.37.q_ref = bf16[8,8,1024]{2,1,0:T(8,128)(2,1)S(1)} all-to-all(bf16[8,8,1024]{2,1,0:T(8,128)(2,1)S(1)} %bitcast.9), channel_id=1, replica_groups=mesh['x'=4,'z'=8,'kvhead'=8] {'z'}, dimensions={0} | all-to-all | bytes 262144 | tf_op jit(solution)/shard_map/all_to_all | solution.py:407
  17.6 0.0 copy-start
  17.6 0.0 copy-start.1
  17.6 0.0 copy-start.4
  17.6 0.0 copy-start.5
  17.6 0.0 copy-start.6
  17.6 2.6 %collective-permute-start.2 = (bf16[8,8,1024]{2,1,0:T(8,128)(2,1)S(1)}, bf16[8,8,1024]{2,1,0:T(8,128)(2,1)S(1)}, u32[]{:S(2)}, u32[]{:S(2)}) collective-permute-start(bf16[8,8,1024]{2,1,0:T(8,128)(2,1)S(1)} %all_to_all.37.q_ref), channel_id=1, source_target_pairs={{0,192},{64,0},{128,64},{192,128},{1,193},{65,1},{129,65},{193,129... | collective-permute-start | bytes 393224 | tf_op jit(solution)/shard_map/ppermute | solution.py:424
  20.2 0.5 collective-permute-start.1
  20.7 0.6 collective-permute-start
  21.3 0.0 copy-done.7
  21.3 0.0 copy-done.8
  21.3 38.4 %first_part.1 = (bf16[4,16,1152]{2,1,0:T(8,128)(2,1)S(1)}, bf16[144,8192]{1,0:T(8,128)(2,1)S(1)}) custom-call(bf16[8,8,1024]{2,1,0:T(8,128)(2,1)S(1)} %all_to_all.37.q_ref, bf16[8192,128]{1,0:T(8,128)(2,1)S(1)} %copy-done.7, bf16[8192,128]{1,0:T(8,128)(2,1)S(1)} %copy-done.8), custom_call_target="tpu_custom_call" | custom-call | flops 4294967296 | bytes 4194304 | tf_op jit(solution)/shard_map/first_part/pallas_call | solution.py:200
  59.7 0.0 copy-done
  59.7 0.0 copy-done.1
  59.7 0.0 copy-done.4
  59.7 0.0 copy-done.5
  59.7 0.0 copy-done.6
  59.7 2.0 suffix_part.1.refs_6_
  61.7 0.0 collective-permute-done.2.refs_2_
  61.7 0.0 collective-permute-done.1.refs_1_
  61.7 0.0 collective-permute-done.refs_0_
  61.7 83.6 %class_part.2 = (bf16[64,1152]{1,0:T(8,128)(2,1)S(1)}, bf16[64,1152]{1,0:T(8,128)(2,1)S(1)}, bf16[64,1152]{1,0:T(8,128)(2,1)S(1)}) custom-call(bf16[8,8,1024]{2,1,0:T(8,128)(2,1)S(1)} %collective-permute-done.refs_0_, bf16[8,8,1024]{2,1,0:T(8,128)(2,1)S(1)} %collective-permute-done.1.refs_1_, bf16[8,8,1024]{2,1,0:T(8,128)(2,1)S(1)} %collective-permute-done.2.refs_2_, ...), custom_call_target="tpu_custom_call" | custom-call | flops 9663676416 | bytes 4194304 | tf_op jit(solution)/shard_map/class_part/pallas_call | solution.py:200
  145.3 1.6 collective-permute-start.3
  146.9 1.7 collective-permute-start.4
  148.6 1.0 collective-permute-start.5
  149.6 28.8 %class_part.3.refs_0_ = bf16[64,1152]{1,0:T(8,128)(2,1)S(1)} custom-call(bf16[8,8,1024]{2,1,0:T(8,128)(2,1)S(1)} %collective-permute-done.refs_0_, bf16[8,8,1024]{2,1,0:T(8,128)(2,1)S(1)} %collective-permute-done.1.refs_1_, bf16[8,8,1024]{2,1,0:T(8,128)(2,1)S(1)} %collective-permute-done.2.refs_2_, bf16[8192,128]{1,0:T(8,128)(2,1)S(1)} %copy-done.7, ...), custom_call_target="tpu_custom_call" | custom-call | flops 3221225472 | bytes 4194304 | tf_op jit(solution)/shard_map/class_part/pallas_call | solution.py:200
  178.4 0.0 copy-start.2
  178.4 0.0 collective-permute-done.3.refs_1_
  178.4 0.0 collective-permute-done.4.refs_2_
  178.4 0.0 collective-permute-done.5.refs_3_
  178.5 0.6 merge_x.1
  179.0 10.5 %all_to_all.38 = bf16[8,8,1152]{2,1,0:T(8,128)(2,1)S(1)} all-to-all(bf16[8,8,1152]{2,1,0:T(8,128)(2,1)S(1)} %bitcast.7), channel_id=1, replica_groups=mesh['x'=4,'z'=8,'kvhead'=8] {'z'}, dimensions={0} | all-to-all | bytes 294912 | tf_op jit(solution)/shard_map/all_to_all | solution.py:407
  189.5 0.2 merge_z.1
  189.8 14.5 %all_to_all.39 = bf16[32,8,1024]{2,1,0:T(8,128)(2,1)S(1)} all-to-all(bf16[32,8,1024]{2,1,0:T(8,128)(2,1)S(1)} %bitcast.5), channel_id=1, replica_groups=mesh['x'=4,'z'=8,'kvhead'=8] {'x','z'}, dimensions={0} | all-to-all | bytes 1048576 | tf_op jit(solution)/shard_map/all_to_all | solution.py:407
  204.3 0.0 copy-done.2
  204.3 0.3 project.1
  204.6 17.5 %all_to_all.40 = bf16[8,32,256]{2,1,0:T(8,128)(2,1)S(1)} all-to-all(bf16[8,32,256]{2,1,0:T(8,128)(2,1)S(1)} %project.1), channel_id=1, replica_groups=mesh['x'=4,'z'=8,'kvhead'=8] {'kvhead'}, dimensions={0} | all-to-all | bytes 262144 | tf_op jit(solution)/shard_map/all_to_all | solution.py:407
  222.1 0.6 reduce_sum.12
  (1 shorter events, 0.0 us)
Async XLA Ops:
  0.0 0.7 copy-start.3
  0.7 20.6 %copy-start.7 = (bf16[8192,128]{1,0:T(8,128)(2,1)S(1)}, bf16[8192,128]{1,0:T(8,128)(2,1)}, u32[]{:S(2)}) copy-start(bf16[8192,128]{1,0:T(8,128)(2,1)} %refs_3_.3) | copy-start | bytes 6291460
  0.7 20.6 %copy-start.8 = (bf16[8192,128]{1,0:T(8,128)(2,1)S(1)}, bf16[8192,128]{1,0:T(8,128)(2,1)}, u32[]{:S(2)}) copy-start(bf16[8192,128]{1,0:T(8,128)(2,1)} %refs_4_.3) | copy-start | bytes 6291460
  17.6 42.1 %copy-start = (bf16[8,1024,128]{2,1,0:T(8,128)(2,1)S(1)}, bf16[8,1024,128]{2,1,0:T(8,128)(2,1)}, u32[]{:S(2)}) copy-start(bf16[8,1024,128]{2,1,0:T(8,128)(2,1)} %keys.1) | copy-start | bytes 6291460
  17.6 42.1 %copy-start.1 = (bf16[8,1024,128]{2,1,0:T(8,128)(2,1)S(1)}, bf16[8,1024,128]{2,1,0:T(8,128)(2,1)}, u32[]{:S(2)}) copy-start(bf16[8,1024,128]{2,1,0:T(8,128)(2,1)} %values.1) | copy-start | bytes 6291460
  17.6 42.1 %copy-start.4 = (bf16[8,1024]{1,0:T(8,128)(2,1)S(1)}, bf16[8,1024]{1,0:T(8,128)(2,1)}, u32[]{:S(2)}) copy-start(bf16[8,1024]{1,0:T(8,128)(2,1)} %q_ref.1) | copy-start | bytes 49156
  17.6 42.1 %copy-start.5 = (s32[256]{0:T(256)S(1)}, s32[256]{0:T(256)}, u32[]{:S(2)}) copy-start(s32[256]{0:T(256)} %lengths_ref.1) | copy-start | bytes 3076
  17.6 42.1 %copy-start.6 = (s32[8]{0:T(128)S(1)}, s32[8]{0:T(128)}, u32[]{:S(2)}) copy-start(s32[8]{0:T(128)} %request_ref.1) | copy-start | bytes 100
  17.6 44.1 %collective-permute-start.2 = (bf16[8,8,1024]{2,1,0:T(8,128)(2,1)S(1)}, bf16[8,8,1024]{2,1,0:T(8,128)(2,1)S(1)}, u32[]{:S(2)}, u32[]{:S(2)}) collective-permute-start(bf16[8,8,1024]{2,1,0:T(8,128)(2,1)S(1)} %all_to_all.37.q_ref), channel_id=1, source_target_pairs={{0,192},{64,0},{128,64},{192,128},{1,193},{65,1},{129,65},{193,129... | collective-permute-start | bytes 393224 | tf_op jit(solution)/shard_map/ppermute | solution.py:424
  20.2 41.6 %collective-permute-start.1 = (bf16[8,8,1024]{2,1,0:T(8,128)(2,1)S(1)}, bf16[8,8,1024]{2,1,0:T(8,128)(2,1)S(1)}, u32[]{:S(2)}, u32[]{:S(2)}) collective-permute-start(bf16[8,8,1024]{2,1,0:T(8,128)(2,1)S(1)} %all_to_all.37.q_ref), channel_id=1, source_target_pairs={{0,128},{64,192},{128,0},{192,64},{1,129},{65,193},{129,1},{193,65... | collective-permute-start | bytes 393224 | tf_op jit(solution)/shard_map/ppermute | solution.py:424
  20.7 41.1 %collective-permute-start = (bf16[8,8,1024]{2,1,0:T(8,128)(2,1)S(1)}, bf16[8,8,1024]{2,1,0:T(8,128)(2,1)S(1)}, u32[]{:S(2)}, u32[]{:S(2)}) collective-permute-start(bf16[8,8,1024]{2,1,0:T(8,128)(2,1)S(1)} %all_to_all.37.q_ref), channel_id=1, source_target_pairs={{0,64},{64,128},{128,192},{192,0},{1,65},{65,129},{129,193},{193,1... | collective-permute-start | bytes 393224 | tf_op jit(solution)/shard_map/ppermute | solution.py:424
  145.3 33.1 %collective-permute-start.3 = (bf16[64,1152]{1,0:T(8,128)(2,1)S(1)}, bf16[64,1152]{1,0:T(8,128)(2,1)S(1)}, u32[]{:S(2)}, u32[]{:S(2)}) collective-permute-start(bf16[64,1152]{1,0:T(8,128)(2,1)S(1)} %get-tuple-element.28), channel_id=1, source_target_pairs={{0,64},{64,128},{128,192},{192,0},{1,65},{65,129},{129,193},{193,1... | collective-permute-start | bytes 442376 | tf_op jit(solution)/shard_map/ppermute | solution.py:424
  146.9 31.5 %collective-permute-start.4 = (bf16[64,1152]{1,0:T(8,128)(2,1)S(1)}, bf16[64,1152]{1,0:T(8,128)(2,1)S(1)}, u32[]{:S(2)}, u32[]{:S(2)}) collective-permute-start(bf16[64,1152]{1,0:T(8,128)(2,1)S(1)} %get-tuple-element.29), channel_id=1, source_target_pairs={{0,128},{64,192},{128,0},{192,64},{1,129},{65,193},{129,1},{193,65... | collective-permute-start | bytes 442376 | tf_op jit(solution)/shard_map/ppermute | solution.py:424
  148.6 29.8 %collective-permute-start.5 = (bf16[64,1152]{1,0:T(8,128)(2,1)S(1)}, bf16[64,1152]{1,0:T(8,128)(2,1)S(1)}, u32[]{:S(2)}, u32[]{:S(2)}) collective-permute-start(bf16[64,1152]{1,0:T(8,128)(2,1)S(1)} %get-tuple-element.30), channel_id=1, source_target_pairs={{0,192},{64,0},{128,64},{192,128},{1,193},{65,1},{129,65},{193,129... | collective-permute-start | bytes 442376 | tf_op jit(solution)/shard_map/ppermute | solution.py:424
  178.4 25.9 %copy-start.2 = (bf16[1024,256]{1,0:T(8,128)(2,1)S(1)}, bf16[1024,256]{1,0:T(8,128)(2,1)}, u32[]{:S(2)}) copy-start(bf16[1024,256]{1,0:T(8,128)(2,1)} %weight_ref.1) | copy-start | bytes 1572868

commit v5 on v4

--- a/solution.py
+++ b/solution.py
@@ -163,7 +163,7 @@
     size = halves * held
     slots = len(q_refs) * size
     here_x = lax.axis_index("x")
-    kinds = [lax.rem(here_x + turn, across) for turn in turns]
+    kinds = [lax.bitwise_xor(here_x, jnp.int32(turn)) for turn in turns]
     for i, kind in enumerate(kinds):
         put_queries(
             rows,
@@ -174,7 +174,7 @@
     def put(outs):
         for out, out_ref, kind in zip(outs, out_refs, kinds, strict=True):
             for n in range(len(q_refs)):
-                at = lax.rem(here_x + across - n - 1, across)
+                at = lax.bitwise_xor(here_x, jnp.int32(n + 1))
                 there = pl.ds(pl.multiple_of(at * size, size), size)
                 out_ref[there, :] = out[n * size : (n + 1) * size]
             there = pl.ds(pl.multiple_of(here_x * size, size), size)
@@ -421,7 +421,7 @@
     across, along, heads = lax.axis_size("x"), lax.axis_size("z"), lax.axis_size("kvhead")
     near = swap(spread(queries, along), "z")
     def to_other_x(array, turn):
-        return lax.ppermute(array, "x", [(i, (i + turn) % across) for i in range(across)])
+        return lax.ppermute(array, "x", [(i, i ^ turn) for i in range(across)])
 
     turns = range(1, across)
     near = near.reshape(along, held, WIDTH)

time: 223 us -> 223 us (level)
  no operation moved by 1% of the time
where the time goes in v5:
time: 223 us
  Pallas kernels  154 us (69%)
  blocking collectives  59.6 us (27%)
  starting transfers between devices  7.34 us (3%)
    pallas_call x3, Pallas kernels, prefix_call(): pl.pallas_call(kernel, in_specs=[vmem] * len(operand_list), out_specs=[vm...  151 us
    all_to_all x4, blocking collectives, swap(): return lax.all_to_all(array, axes, split_axis=0, concat_axis=0, tiled=True)  59.6 us
    ppermute x6, starting transfers between devices, to_other_x(): return lax.ppermute(array, 'x', [(i, i ^ turn) for i in range(across)])  7.34 us
  transfers between devices with their start and end apart: 6, of which 0 were waited for; matrix products, arithmetic and copies ran while one was open for 0% of the time, Pallas kernels for 31%

profile of v5, /device:TPU:1, one launch (start us, length us, event | category | flops | bytes accessed | tf_op | source)
XLA Modules:
  0.0 222.7 jit_solution(784980185411748248)
XLA Ops:
  0.0 0.0 copy-start.3
  0.0 0.7 copy-done.3
  0.7 0.0 copy-start.7
  0.7 0.0 copy-start.8
  0.7 16.8 %all_to_all.37.q_ref = bf16[8,8,1024]{2,1,0:T(8,128)(2,1)S(1)} all-to-all(bf16[8,8,1024]{2,1,0:T(8,128)(2,1)S(1)} %bitcast.9), channel_id=1, replica_groups=mesh['x'=4,'z'=8,'kvhead'=8] {'z'}, dimensions={0} | all-to-all | bytes 262144 | tf_op jit(solution)/shard_map/all_to_all | solution.py:407
  17.6 0.0 copy-start
  17.6 0.0 copy-start.1
  17.6 0.0 copy-start.4
  17.6 0.0 copy-start.5
  17.6 0.0 copy-start.6
  17.6 2.6 %collective-permute-start.2 = (bf16[8,8,1024]{2,1,0:T(8,128)(2,1)S(1)}, bf16[8,8,1024]{2,1,0:T(8,128)(2,1)S(1)}, u32[]{:S(2)}, u32[]{:S(2)}) collective-permute-start(bf16[8,8,1024]{2,1,0:T(8,128)(2,1)S(1)} %all_to_all.37.q_ref), channel_id=1, source_target_pairs={{0,192},{64,128},{128,64},{192,0},{1,193},{65,129},{129,65},{193,1... | collective-permute-start | bytes 393224 | tf_op jit(solution)/shard_map/ppermute | solution.py:424
  20.2 0.5 collective-permute-start.1
  20.7 0.3 collective-permute-start
  20.9 0.0 copy-done.7
  20.9 0.0 copy-done.8
  21.0 38.4 %first_part.1 = (bf16[4,16,1152]{2,1,0:T(8,128)(2,1)S(1)}, bf16[144,8192]{1,0:T(8,128)(2,1)S(1)}) custom-call(bf16[8,8,1024]{2,1,0:T(8,128)(2,1)S(1)} %all_to_all.37.q_ref, bf16[8192,128]{1,0:T(8,128)(2,1)S(1)} %copy-done.7, bf16[8192,128]{1,0:T(8,128)(2,1)S(1)} %copy-done.8), custom_call_target="tpu_custom_call" | custom-call | flops 4294967296 | bytes 4194304 | tf_op jit(solution)/shard_map/first_part/pallas_call | solution.py:200
  59.3 0.0 copy-done
  59.3 0.0 copy-done.1
  59.3 0.0 copy-done.4
  59.3 0.0 copy-done.5
  59.4 0.0 copy-done.6
  59.4 2.0 suffix_part.1.refs_6_
  61.4 0.0 collective-permute-done.2.refs_2_
  61.4 0.0 collective-permute-done.1.refs_1_
  61.4 0.0 collective-permute-done.refs_0_
  61.4 83.9 %class_part.2 = (bf16[64,1152]{1,0:T(8,128)(2,1)S(1)}, bf16[64,1152]{1,0:T(8,128)(2,1)S(1)}, bf16[64,1152]{1,0:T(8,128)(2,1)S(1)}) custom-call(bf16[8,8,1024]{2,1,0:T(8,128)(2,1)S(1)} %collective-permute-done.refs_0_, bf16[8,8,1024]{2,1,0:T(8,128)(2,1)S(1)} %collective-permute-done.1.refs_1_, bf16[8,8,1024]{2,1,0:T(8,128)(2,1)S(1)} %collective-permute-done.2.refs_2_, ...), custom_call_target="tpu_custom_call" | custom-call | flops 9663676416 | bytes 4194304 | tf_op jit(solution)/shard_map/class_part/pallas_call | solution.py:200
  145.3 1.3 collective-permute-start.3
  146.6 2.5 %collective-permute-start.4 = (bf16[64,1152]{1,0:T(8,128)(2,1)S(1)}, bf16[64,1152]{1,0:T(8,128)(2,1)S(1)}, u32[]{:S(2)}, u32[]{:S(2)}) collective-permute-start(bf16[64,1152]{1,0:T(8,128)(2,1)S(1)} %get-tuple-element.29), channel_id=1, source_target_pairs={{0,128},{64,192},{128,0},{192,64},{1,129},{65,193},{129,1},{193,65... | collective-permute-start | bytes 442376 | tf_op jit(solution)/shard_map/ppermute | solution.py:424
  149.1 0.3 collective-permute-start.5
  149.3 28.7 %class_part.3.refs_0_ = bf16[64,1152]{1,0:T(8,128)(2,1)S(1)} custom-call(bf16[8,8,1024]{2,1,0:T(8,128)(2,1)S(1)} %collective-permute-done.refs_0_, bf16[8,8,1024]{2,1,0:T(8,128)(2,1)S(1)} %collective-permute-done.1.refs_1_, bf16[8,8,1024]{2,1,0:T(8,128)(2,1)S(1)} %collective-permute-done.2.refs_2_, bf16[8192,128]{1,0:T(8,128)(2,1)S(1)} %copy-done.7, ...), custom_call_target="tpu_custom_call" | custom-call | flops 3221225472 | bytes 4194304 | tf_op jit(solution)/shard_map/class_part/pallas_call | solution.py:200
  178.1 0.0 copy-start.2
  178.1 0.0 collective-permute-done.3.refs_1_
  178.1 0.0 collective-permute-done.4.refs_2_
  178.1 0.0 collective-permute-done.5.refs_3_
  178.1 0.6 merge_x.1
  178.7 10.5 %all_to_all.38 = bf16[8,8,1152]{2,1,0:T(8,128)(2,1)S(1)} all-to-all(bf16[8,8,1152]{2,1,0:T(8,128)(2,1)S(1)} %bitcast.7), channel_id=1, replica_groups=mesh['x'=4,'z'=8,'kvhead'=8] {'z'}, dimensions={0} | all-to-all | bytes 294912 | tf_op jit(solution)/shard_map/all_to_all | solution.py:407
  189.2 0.2 merge_z.1
  189.5 14.5 %all_to_all.39 = bf16[32,8,1024]{2,1,0:T(8,128)(2,1)S(1)} all-to-all(bf16[32,8,1024]{2,1,0:T(8,128)(2,1)S(1)} %bitcast.5), channel_id=1, replica_groups=mesh['x'=4,'z'=8,'kvhead'=8] {'x','z'}, dimensions={0} | all-to-all | bytes 1048576 | tf_op jit(solution)/shard_map/all_to_all | solution.py:407
  204.0 0.0 copy-done.2
  204.0 0.3 project.1
  204.3 17.8 %all_to_all.40 = bf16[8,32,256]{2,1,0:T(8,128)(2,1)S(1)} all-to-all(bf16[8,32,256]{2,1,0:T(8,128)(2,1)S(1)} %project.1), channel_id=1, replica_groups=mesh['x'=4,'z'=8,'kvhead'=8] {'kvhead'}, dimensions={0} | all-to-all | bytes 262144 | tf_op jit(solution)/shard_map/all_to_all | solution.py:407
  222.1 0.6 reduce_sum.12
  (1 shorter events, 0.0 us)
Async XLA Ops:
  0.0 0.7 copy-start.3
  0.7 20.2 %copy-start.7 = (bf16[8192,128]{1,0:T(8,128)(2,1)S(1)}, bf16[8192,128]{1,0:T(8,128)(2,1)}, u32[]{:S(2)}) copy-start(bf16[8192,128]{1,0:T(8,128)(2,1)} %refs_3_.3) | copy-start | bytes 6291460
  0.7 20.2 %copy-start.8 = (bf16[8192,128]{1,0:T(8,128)(2,1)S(1)}, bf16[8192,128]{1,0:T(8,128)(2,1)}, u32[]{:S(2)}) copy-start(bf16[8192,128]{1,0:T(8,128)(2,1)} %refs_4_.3) | copy-start | bytes 6291460
  17.6 41.7 %copy-start = (bf16[8,1024,128]{2,1,0:T(8,128)(2,1)S(1)}, bf16[8,1024,128]{2,1,0:T(8,128)(2,1)}, u32[]{:S(2)}) copy-start(bf16[8,1024,128]{2,1,0:T(8,128)(2,1)} %keys.1) | copy-start | bytes 6291460
  17.6 41.7 %copy-start.1 = (bf16[8,1024,128]{2,1,0:T(8,128)(2,1)S(1)}, bf16[8,1024,128]{2,1,0:T(8,128)(2,1)}, u32[]{:S(2)}) copy-start(bf16[8,1024,128]{2,1,0:T(8,128)(2,1)} %values.1) | copy-start | bytes 6291460
  17.6 41.8 %copy-start.4 = (bf16[8,1024]{1,0:T(8,128)(2,1)S(1)}, bf16[8,1024]{1,0:T(8,128)(2,1)}, u32[]{:S(2)}) copy-start(bf16[8,1024]{1,0:T(8,128)(2,1)} %q_ref.1) | copy-start | bytes 49156
  17.6 41.8 %copy-start.5 = (s32[256]{0:T(256)S(1)}, s32[256]{0:T(256)}, u32[]{:S(2)}) copy-start(s32[256]{0:T(256)} %lengths_ref.1) | copy-start | bytes 3076
  17.6 41.8 %copy-start.6 = (s32[8]{0:T(128)S(1)}, s32[8]{0:T(128)}, u32[]{:S(2)}) copy-start(s32[8]{0:T(128)} %request_ref.1) | copy-start | bytes 100
  17.6 43.8 %collective-permute-start.2 = (bf16[8,8,1024]{2,1,0:T(8,128)(2,1)S(1)}, bf16[8,8,1024]{2,1,0:T(8,128)(2,1)S(1)}, u32[]{:S(2)}, u32[]{:S(2)}) collective-permute-start(bf16[8,8,1024]{2,1,0:T(8,128)(2,1)S(1)} %all_to_all.37.q_ref), channel_id=1, source_target_pairs={{0,192},{64,128},{128,64},{192,0},{1,193},{65,129},{129,65},{193,1... | collective-permute-start | bytes 393224 | tf_op jit(solution)/shard_map/ppermute | solution.py:424
  20.2 41.2 %collective-permute-start.1 = (bf16[8,8,1024]{2,1,0:T(8,128)(2,1)S(1)}, bf16[8,8,1024]{2,1,0:T(8,128)(2,1)S(1)}, u32[]{:S(2)}, u32[]{:S(2)}) collective-permute-start(bf16[8,8,1024]{2,1,0:T(8,128)(2,1)S(1)} %all_to_all.37.q_ref), channel_id=1, source_target_pairs={{0,128},{64,192},{128,0},{192,64},{1,129},{65,193},{129,1},{193,65... | collective-permute-start | bytes 393224 | tf_op jit(solution)/shard_map/ppermute | solution.py:424
  20.7 40.7 %collective-permute-start = (bf16[8,8,1024]{2,1,0:T(8,128)(2,1)S(1)}, bf16[8,8,1024]{2,1,0:T(8,128)(2,1)S(1)}, u32[]{:S(2)}, u32[]{:S(2)}) collective-permute-start(bf16[8,8,1024]{2,1,0:T(8,128)(2,1)S(1)} %all_to_all.37.q_ref), channel_id=1, source_target_pairs={{0,64},{64,0},{128,192},{192,128},{1,65},{65,1},{129,193},{193,129... | collective-permute-start | bytes 393224 | tf_op jit(solution)/shard_map/ppermute | solution.py:424
  145.3 32.8 %collective-permute-start.3 = (bf16[64,1152]{1,0:T(8,128)(2,1)S(1)}, bf16[64,1152]{1,0:T(8,128)(2,1)S(1)}, u32[]{:S(2)}, u32[]{:S(2)}) collective-permute-start(bf16[64,1152]{1,0:T(8,128)(2,1)S(1)} %get-tuple-element.28), channel_id=1, source_target_pairs={{0,64},{64,0},{128,192},{192,128},{1,65},{65,1},{129,193},{193,129... | collective-permute-start | bytes 442376 | tf_op jit(solution)/shard_map/ppermute | solution.py:424
  146.6 31.5 %collective-permute-start.4 = (bf16[64,1152]{1,0:T(8,128)(2,1)S(1)}, bf16[64,1152]{1,0:T(8,128)(2,1)S(1)}, u32[]{:S(2)}, u32[]{:S(2)}) collective-permute-start(bf16[64,1152]{1,0:T(8,128)(2,1)S(1)} %get-tuple-element.29), channel_id=1, source_target_pairs={{0,128},{64,192},{128,0},{192,64},{1,129},{65,193},{129,1},{193,65... | collective-permute-start | bytes 442376 | tf_op jit(solution)/shard_map/ppermute | solution.py:424
  149.1 29.0 %collective-permute-start.5 = (bf16[64,1152]{1,0:T(8,128)(2,1)S(1)}, bf16[64,1152]{1,0:T(8,128)(2,1)S(1)}, u32[]{:S(2)}, u32[]{:S(2)}) collective-permute-start(bf16[64,1152]{1,0:T(8,128)(2,1)S(1)} %get-tuple-element.30), channel_id=1, source_target_pairs={{0,192},{64,128},{128,64},{192,0},{1,193},{65,129},{129,65},{193,1... | collective-permute-start | bytes 442376 | tf_op jit(solution)/shard_map/ppermute | solution.py:424
  178.1 25.9 %copy-start.2 = (bf16[1024,256]{1,0:T(8,128)(2,1)S(1)}, bf16[1024,256]{1,0:T(8,128)(2,1)}, u32[]{:S(2)}) copy-start(bf16[1024,256]{1,0:T(8,128)(2,1)} %weight_ref.1) | copy-start | bytes 1572868
